TPU v7x, 512 devices: a whole 4x8x8 slice. The times are simulated.
512 devices in a mesh: pulse: 64 (over z, y), chan: 8 (over x, core).
Axes of the slice: x: 4, y: 8, z: 8, core: 2. Of those that a mesh axis runs over, the one named last changes fastest.
Arguments:
- echoes: bfloat16 [2, 8, 4096, 4096], P(None, 'chan', 'pulse'), may hold values from -6 to 6
- range_phase: float32 [512], replicated, may hold values from -3.140625 to 3.140625
- azimuth_rate: float32 [512], P('pulse'), may hold values from 1 to 4
- band_lo: int32 [64], P('pulse'), may hold values from 0 to 504, as said below
- band_hi: int32 [64], P('pulse'), may hold values from 8 to 512, as said below
- band_map: int32 [8], replicated, may hold values from 0 to 7, each once
- recon_filter: bfloat16 [8, 8, 2, 4096], replicated, may hold values from -1.5 to 1.5
Outputs:
- focused: float32 [2, 512, 32768], P(None, 'pulse', 'chan')
Inputs may be any that keep to these rules, and one draw needn't show every extreme that they name: band_lo[b] lies in [b * 8 - 8, b * 8] and in the slab; the last block's band begins at the block; in some block strictly between the first and the last the band begins 8 bins before the block. band_hi[b] lies in [b * 8 + 8, b * 8 + 2 * 8] and in the slab; the first block's band ends at the block's end; in the same block as above the band ends 8 bins after it. `band_map`: a permutation.
All inputs are finite; a program needn't handle non-finite values.
Results may differ from a plain program's by a relative error of at most 0.0037.
Values may be sent and summed in bfloat16 or wider, within the bound.
No kernel may reach another device: no remote copies, remote signals or barrier semaphores. Data moves between devices by JAX's collectives and lax.ppermute only.
A program may use at most 128 MiB of HBM per device.

v0:
```python
import math

import jax
import jax.numpy as jnp
import numpy as np
from jax import lax
from jax.experimental import pallas as pl
from jax.experimental.pallas import tpu as pltpu
from jax.sharding import PartitionSpec as P

NS = 4096
RB_DEV = 8
MIGRATION = 7
PULSES = 4096
NR = 512
CHANS = 8
SPECTRUM = 32768
N_PULSE = 64

RADIX = 4
FOLD = NS // RADIX
LANES = 128
ROWS = PULSES // LANES
OWN = ROWS // CHANS
PULSES_DEV = PULSES // N_PULSE
curvature = 300.0

f32 = jnp.float32
bf16 = jnp.bfloat16


def split_np(values):
    high = np.asarray(values, np.float32).astype(bf16)
    low = (values - high.astype(np.float64)).astype(np.float32).astype(bf16)
    return high, low


def range_tables():
    tables = []
    sample = np.arange(FOLD)
    for rho in range(RADIX):
        bins = np.array([8 * block + 4 * h + rho for h in range(2) for block in range(N_PULSE)])
        angle = (bins[:, None] * sample[None, :]) % NS * (2.0 * math.pi / NS)
        tables.append(np.concatenate([np.cos(angle), np.sin(angle)], axis=0))
    return np.stack(tables).astype(np.float32).astype(bf16)


def row_tables():
    digit = np.arange(ROWS)
    angle = (digit[:, None] * digit[None, :]) % ROWS * (2.0 * math.pi / ROWS)
    eye = np.eye(RB_DEV)
    cos_hi, cos_lo = split_np(np.kron(np.cos(angle), eye))
    sin_hi, sin_lo = split_np(np.kron(np.sin(angle), eye))
    return np.concatenate([cos_hi, sin_hi, cos_lo, sin_lo], axis=0)


def lane_tables():
    digit = np.arange(LANES)
    angle = (digit[:, None] * digit[None, :]) % LANES * (2.0 * math.pi / LANES)
    cos_m, sin_m = np.cos(angle), np.sin(angle)
    high, low = split_np(np.block([[cos_m, -sin_m], [sin_m, cos_m]]))
    return np.concatenate([high, low], axis=1)


def twiddle_tables():
    angle = np.arange(ROWS)[:, None] * np.arange(LANES)[None, :] * (2.0 * math.pi / PULSES)
    angle = np.repeat(angle, RB_DEV, axis=0)
    return np.concatenate([np.cos(angle), np.sin(angle)], axis=1).astype(np.float32)


def dot(left, right):
    return jnp.dot(left, right, preferred_element_type=f32)


def split(values):
    high = values.astype(bf16)
    return high, (values - high.astype(f32)).astype(bf16)


def lane_index(shape):
    return lax.broadcasted_iota(jnp.int32, shape, 1)


def compress_kernel(echo_ref, table_ref, out_ref, folded, bins):
    rho = pl.program_id(0)

    def quarters(part):
        return [
            echo_ref[part, 0, :, a * FOLD : (a + 1) * FOLD].astype(f32) for a in range(RADIX)
        ]

    def put(part, values):
        high, low = split(values)
        folded[part * 64 : part * 64 + 64, :] = high
        folded[128 + part * 64 : 128 + part * 64 + 64, :] = low

    for residue in range(RADIX):

        @pl.when(rho == residue)
        def _():
            re0, re1, re2, re3 = quarters(0)
            im0, im1, im2, im3 = quarters(1)
            if residue == 0:
                put(0, (re0 + re2) + (re1 + re3))
                put(1, (im0 + im2) + (im1 + im3))
            elif residue == 1:
                put(0, (re0 - re2) + (im1 - im3))
                put(1, (im0 - im2) - (re1 - re3))
            elif residue == 2:
                put(0, (re0 + re2) - (re1 + re3))
                put(1, (im0 + im2) - (im1 + im3))
            else:
                put(0, (re0 - re2) - (im1 - im3))
                put(1, (im0 - im2) + (re1 - re3))
            sums = lax.dot_general(
                table_ref[0], folded[...], (((1,), (1,)), ((), ())), preferred_element_type=f32
            )
            sums = sums[:, :LANES] + sums[:, LANES:]
            cos_sum, sin_sum = sums[:128], sums[128:]
            sign = jnp.where(lane_index((128, LANES)) < 64, 1.0, -1.0)
            comp = cos_sum + sign * pltpu.roll(sin_sum, 64, 1)
            for h in range(2):
                bins[pl.ds(4 * h + residue, N_PULSE, stride=RB_DEV), :] = comp[
                    h * N_PULSE : (h + 1) * N_PULSE
                ]

    @pl.when(rho == RADIX - 1)
    def _():
        own = bins[...].astype(bf16).reshape(N_PULSE, RB_DEV, LANES)
        edge = jnp.zeros((1, RB_DEV, LANES), bf16)
        out_ref[0:1, :, 0:LANES] = edge
        out_ref[1:N_PULSE, :, 0:LANES] = own[: N_PULSE - 1]
        out_ref[:, :, LANES : 2 * LANES] = own
        out_ref[0 : N_PULSE - 1, :, 2 * LANES :] = own[1:]
        out_ref[N_PULSE - 1 :, :, 2 * LANES :] = edge


def compress(echoes, tables):
    return pl.pallas_call(
        compress_kernel,
        grid=(RADIX,),
        in_specs=[
            pl.BlockSpec((2, 1, PULSES_DEV, NS), lambda rho: (0, 0, 0, 0)),
            pl.BlockSpec((1, 256, FOLD), lambda rho: (rho, 0, 0)),
        ],
        out_specs=pl.BlockSpec((N_PULSE, RB_DEV, 3 * LANES), lambda rho: (0, 0, 0)),
        out_shape=jax.ShapeDtypeStruct((N_PULSE, RB_DEV, 3 * LANES), bf16),
        scratch_shapes=[pltpu.VMEM((256, FOLD), bf16), pltpu.VMEM((NR, LANES), f32)],
        compiler_params=pltpu.CompilerParams(vmem_limit_bytes=32 << 20),
        cost_estimate=pl.CostEstimate(
            flops=2 * RADIX * 256 * 256 * FOLD, bytes_accessed=4 << 20, transcendentals=0
        ),
        name="compress",
    )(echoes, tables)


def spectra_kernel(turned_ref, rows_ref, lanes_ref, twiddle_ref, gain_ref, out_ref):
    low_half = lane_index((256, LANES)) < 64
    tw_cos, tw_sin = twiddle_ref[:, :LANES], twiddle_ref[:, LANES:]
    table_hi, table_lo = lanes_ref[:, :256], lanes_ref[:, 256:]
    for group in range(3):
        taken = turned_ref[:, :, group * LANES : (group + 1) * LANES].astype(f32)
        pairs = taken.reshape(ROWS, 2, RB_DEV, LANES)
        even = pairs[:, 0].reshape(256, LANES)
        odd = pairs[:, 1].reshape(256, LANES)
        real_x = jnp.where(low_half, even, pltpu.roll(odd, 64, 1))
        imag_x = jnp.where(low_half, pltpu.roll(even, 64, 1), odd)
        samples = jnp.concatenate([real_x, imag_x], axis=1).astype(bf16)
        turned = dot(rows_ref[...], samples)
        cos_sum = turned[0:256] + turned[512:768]
        sin_sum = turned[256:512] + turned[768:1024]
        real_y = cos_sum[:, :LANES] + sin_sum[:, LANES:]
        imag_y = cos_sum[:, LANES:] - sin_sum[:, :LANES]
        real_z = real_y * tw_cos + imag_y * tw_sin
        imag_z = imag_y * tw_cos - real_y * tw_sin
        gain_re = gain_ref[0, group][None]
        gain_im = gain_ref[1, group][None]
        real_z = real_z.reshape(ROWS, RB_DEV, LANES)
        imag_z = imag_z.reshape(ROWS, RB_DEV, LANES)
        real_w = (real_z * gain_re - imag_z * gain_im).reshape(256, LANES)
        imag_w = (imag_z * gain_re + real_z * gain_im).reshape(256, LANES)
        high, low = split(jnp.concatenate([real_w, imag_w], axis=1))
        result = dot(high, table_hi) + (dot(low, table_hi) + dot(high, table_lo))
        out_ref[:, group * 32 : (group + 1) * 32, :] = result.astype(bf16).reshape(
            CHANS, 32, 256
        )


def spectra(turned, rows_table, lanes_table, twiddle, gain):
    return pl.pallas_call(
        spectra_kernel,
        out_shape=jax.ShapeDtypeStruct((CHANS, 96, 256), bf16),
        compiler_params=pltpu.CompilerParams(vmem_limit_bytes=32 << 20),
        cost_estimate=pl.CostEstimate(
            flops=6 * 256 * 256 * 1792, bytes_accessed=2 << 20, transcendentals=0
        ),
        name="spectra",
    )(turned, rows_table, lanes_table, twiddle, gain)


def prepare_kernel(
    scalars, rate_ref, filter_ref, filt_ref, cos_ref, sin_ref, base_ref, lanes_ref, twiddle_ref
):
    chan = scalars[CHANS]
    block = scalars[CHANS + 1]
    shape = (OWN * RB_DEV, LANES)
    row = lax.broadcasted_iota(jnp.int32, shape, 0)
    lane = lax.broadcasted_iota(jnp.int32, shape, 1)
    doppler_bin = 32 * lane + OWN * chan + lax.shift_right_logical(row, 3)
    q = jnp.bitwise_and(row, 7)
    bins = (block * RB_DEV + q).astype(f32)
    slope = 0.5 + 0.5 * bins / NR
    place = (RB_DEV + q).astype(f32)
    rates = jnp.concatenate([rate_ref[...]] * OWN, axis=0)
    for k in range(CHANS):
        doppler = (scalars[k] * PULSES + doppler_bin).astype(f32) / SPECTRUM - 0.5
        spread = 2.0 * jnp.square(2.0 * doppler) * slope - 1.0
        base_ref[k] = place - (place + MIGRATION * spread)
        phase = -curvature * jnp.square(doppler) / rates
        cos_ref[k] = jnp.cos(phase)
        sin_ref[k] = jnp.sin(phase)
    pick_x = lax.broadcasted_iota(jnp.int32, (1024, LANES), 0)
    pick_y = lax.broadcasted_iota(jnp.int32, (1024, LANES), 1)
    wanted = 32 * jnp.bitwise_and(pick_y, 31) + OWN * chan + lax.shift_right_logical(pick_y, 5)
    pick = jnp.where(pick_x == wanted, 1.0, 0.0).astype(bf16)
    quarter = lax.shift_right_logical(lane_index((128, LANES)), 5)
    picked = [dot(filter_ref[:, 1024 * t : 1024 * (t + 1)], pick) for t in range(4)]
    for digit in range(OWN):
        total = jnp.zeros((128, LANES), f32)
        for t in range(4):
            moved = picked[t]
            if t != digit:
                moved = pltpu.roll(moved, (32 * (t - digit)) % LANES, 1)
            total = jnp.where(quarter == t, moved, total)
        filt_ref[digit] = total
    square = (LANES, LANES)
    j_hi = lax.broadcasted_iota(jnp.int32, square, 0)
    m_lo = lax.broadcasted_iota(jnp.int32, square, 1)
    turns = jnp.bitwise_and(8 * j_hi * m_lo + j_hi * chan, 1023)
    angle = turns.astype(f32) * (2.0 * math.pi / 1024)
    cos_hi, cos_lo = split(jnp.cos(angle))
    sin_hi, sin_lo = split(jnp.sin(angle))
    for at, (cos_m, sin_m) in enumerate(((cos_hi, sin_hi), (cos_lo, sin_lo))):
        left, mid, right = 256 * at, 256 * at + LANES, 256 * at + 256
        lanes_ref[:LANES, left:mid] = cos_m
        lanes_ref[:LANES, mid:right] = sin_m
        lanes_ref[LANES:, left:mid] = -sin_m
        lanes_ref[LANES:, mid:right] = cos_m
    small = (ROWS, LANES)
    j_lo = lax.broadcasted_iota(jnp.int32, small, 0)
    m_low = lax.broadcasted_iota(jnp.int32, small, 1)
    angle = (j_lo * (8 * m_low + chan)).astype(f32) * (2.0 * math.pi / SPECTRUM)
    scale = 1.0 / math.sqrt(SPECTRUM)
    for at, values in enumerate((jnp.cos(angle) * scale, jnp.sin(angle) * scale)):
        full = jnp.broadcast_to(values[:, None, :], (ROWS, RB_DEV, LANES)).reshape(256, LANES)
        twiddle_ref[:, at * LANES : (at + 1) * LANES] = full


def prepare(scalars, rates, filters):
    vmem = pl.BlockSpec(memory_space=pltpu.VMEM)
    return pl.pallas_call(
        prepare_kernel,
        in_specs=[pl.BlockSpec(memory_space=pltpu.SMEM), vmem, vmem],
        out_shape=(
            jax.ShapeDtypeStruct((OWN, 128, LANES), f32),
            jax.ShapeDtypeStruct((CHANS, OWN * RB_DEV, LANES), f32),
            jax.ShapeDtypeStruct((CHANS, OWN * RB_DEV, LANES), f32),
            jax.ShapeDtypeStruct((CHANS, OWN * RB_DEV, LANES), f32),
            jax.ShapeDtypeStruct((256, 512), bf16),
            jax.ShapeDtypeStruct((256, 256), f32),
        ),
        compiler_params=pltpu.CompilerParams(vmem_limit_bytes=32 << 20),
        cost_estimate=pl.CostEstimate(
            flops=1 << 29, bytes_accessed=2 << 20, transcendentals=1 << 18
        ),
        name="prepare",
    )(scalars, rates, filters)


def fft8(values):
    def add(u, v):
        return (u[0] + v[0], u[1] + v[1])

    def sub(u, v):
        return (u[0] - v[0], u[1] - v[1])

    def times_i(u):
        return (-u[1], u[0])

    half = math.sqrt(0.5)

    def fft4(v0, v1, v2, v3):
        e0, e1 = add(v0, v2), sub(v0, v2)
        o0, o1 = add(v1, v3), times_i(sub(v1, v3))
        return [add(e0, o0), add(e1, o1), sub(e0, o0), sub(e1, o1)]

    even = fft4(values[0], values[2], values[4], values[6])
    odd = fft4(values[1], values[3], values[5], values[7])
    odd[1] = ((odd[1][0] - odd[1][1]) * half, (odd[1][0] + odd[1][1]) * half)
    odd[2] = times_i(odd[2])
    odd[3] = ((-odd[3][0] - odd[3][1]) * half, (odd[3][0] - odd[3][1]) * half)
    return [add(e, o) for e, o in zip(even, odd)] + [sub(e, o) for e, o in zip(even, odd)]


def merge_kernel(
    scalars, gathered_ref, filt_ref, cos_ref, sin_ref, base_ref, out_ref, wide, merged, bands
):
    wide[...] = gathered_ref[...].astype(f32)

    def one_band(k, carry):
        band = scalars[k]
        for digit in range(OWN):
            rows = slice(digit * RB_DEV, (digit + 1) * RB_DEV)
            filters = filt_ref[digit, pl.ds(pl.multiple_of(k * 16, 16), 16), :]
            sums_re = [None] * 3
            sums_im = [None] * 3
            for c in range(CHANS):
                f_re = jnp.broadcast_to(filters[2 * c : 2 * c + 1], (RB_DEV, LANES))
                f_im = jnp.broadcast_to(filters[2 * c + 1 : 2 * c + 2], (RB_DEV, LANES))
                for group in range(3):
                    at = group * 32 + digit * RB_DEV
                    s_re = wide[c, at : at + RB_DEV, :LANES]
                    s_im = wide[c, at : at + RB_DEV, LANES:]
                    part_re = f_re * s_re - f_im * s_im
                    part_im = f_re * s_im + f_im * s_re
                    sums_re[group] = part_re if c == 0 else sums_re[group] + part_re
                    sums_im[group] = part_im if c == 0 else sums_im[group] + part_im
            for group in range(3):
                span = slice(group * RB_DEV, (group + 1) * RB_DEV)
                merged[digit, 0, span, :] = sums_re[group]
                merged[digit, 1, span, :] = sums_im[group]
            base = base_ref[k, rows, :]
            moved_re = None
            for step in range(-MIGRATION, MIGRATION + 1):
                weight = jnp.maximum(0.0, 1.0 - jnp.abs(base + float(step)))
                first = RB_DEV + step
                part_re = weight * merged[digit, 0, first : first + RB_DEV, :]
                part_im = weight * merged[digit, 1, first : first + RB_DEV, :]
                moved_re = part_re if moved_re is None else moved_re + part_re
                moved_im = part_im if step == -MIGRATION else moved_im + part_im
            cos_p = cos_ref[k, rows, :]
            sin_p = sin_ref[k, rows, :]
            bands[band, 0, rows, :] = moved_re * cos_p - moved_im * sin_p
            bands[band, 1, rows, :] = moved_im * cos_p + moved_re * sin_p
        return carry

    lax.fori_loop(0, CHANS, one_band, 0)
    for half in range(OWN * RB_DEV // 16):
        rows = slice(half * 16, half * 16 + 16)
        results = fft8([(bands[k, 0, rows, :], bands[k, 1, rows, :]) for k in range(CHANS)])
        for a in range(CHANS):
            out_ref[a, rows, :LANES] = results[a][0].astype(bf16)
            out_ref[a, rows, LANES:] = results[a][1].astype(bf16)


def merge(scalars, gathered, filt, cos_p, sin_p, base):
    vmem = pl.BlockSpec(memory_space=pltpu.VMEM)
    return pl.pallas_call(
        merge_kernel,
        in_specs=[pl.BlockSpec(memory_space=pltpu.SMEM)] + [vmem] * 5,
        out_shape=jax.ShapeDtypeStruct((CHANS, OWN * RB_DEV, 256), bf16),
        scratch_shapes=[
            pltpu.VMEM((CHANS, 96, 256), f32),
            pltpu.VMEM((OWN, 2, 3 * RB_DEV, LANES), f32),
            pltpu.VMEM((CHANS, 2, OWN * RB_DEV, LANES), f32),
        ],
        compiler_params=pltpu.CompilerParams(vmem_limit_bytes=32 << 20),
        cost_estimate=pl.CostEstimate(flops=1 << 24, bytes_accessed=2 << 20, transcendentals=0),
        name="merge",
    )(scalars, gathered, filt, cos_p, sin_p, base)


def image_kernel(combined_ref, rows_ref, lanes_ref, twiddle_ref, out_ref):
    combined = combined_ref[...].reshape(256, 256)
    turned = dot(combined, lanes_ref[...])
    turned = turned[:, :256] + turned[:, 256:]
    real_y, imag_y = turned[:, :LANES], turned[:, LANES:]
    tw_cos, tw_sin = twiddle_ref[:, :LANES], twiddle_ref[:, LANES:]
    real_z = real_y * tw_cos - imag_y * tw_sin
    imag_z = imag_y * tw_cos + real_y * tw_sin
    high, low = split(jnp.concatenate([real_z, imag_z], axis=1))
    wide = dot(rows_ref[...], high)
    rest = dot(rows_ref[0:512], low)
    cos_sum = wide[0:256] + (wide[512:768] + rest[0:256])
    sin_sum = wide[256:512] + (wide[768:1024] + rest[256:512])
    real_x = cos_sum[:, :LANES] - sin_sum[:, LANES:]
    imag_x = cos_sum[:, LANES:] + sin_sum[:, :LANES]
    for m_hi in range(ROWS):
        rows = slice(m_hi * RB_DEV, (m_hi + 1) * RB_DEV)
        cols = slice(m_hi * LANES, (m_hi + 1) * LANES)
        out_ref[0, :, cols] = real_x[rows]
        out_ref[1, :, cols] = imag_x[rows]


def image(combined, rows_table, lanes_table, twiddle):
    return pl.pallas_call(
        image_kernel,
        out_shape=jax.ShapeDtypeStruct((2, RB_DEV, PULSES), f32),
        compiler_params=pltpu.CompilerParams(vmem_limit_bytes=32 << 20),
        cost_estimate=pl.CostEstimate(
            flops=2 * 256 * 256 * 2048, bytes_accessed=2 << 20, transcendentals=0
        ),
        name="image",
    )(combined, rows_table, lanes_table, twiddle)


def window_gain(range_phase, band_lo, band_hi, block_index):
    slab_bins = block_index * RB_DEV - RB_DEV + lax.iota(jnp.int32, 3 * RB_DEV)
    inside = (slab_bins >= band_lo[0]) & (slab_bins < band_hi[0])
    scale = jnp.where(inside, 1.0 / math.sqrt(NS * PULSES), 0.0)
    phase = lax.dynamic_slice(
        jnp.pad(range_phase, (RB_DEV, RB_DEV)), (block_index * RB_DEV,), (3 * RB_DEV,)
    )
    gain = jnp.stack([scale * jnp.cos(phase), scale * jnp.sin(phase)])
    return jnp.broadcast_to(gain.reshape(2, 3, RB_DEV, 1), (2, 3, RB_DEV, LANES))


def per_device(echoes, range_phase, azimuth_rate, band_lo, band_hi, band_map, recon_filter):
    block_index = lax.axis_index("pulse").astype(jnp.int32)
    own_index = lax.axis_index("chan").astype(jnp.int32)
    scalars = jnp.concatenate([band_map, jnp.stack([own_index, block_index])])
    rows_table = jnp.asarray(row_tables())
    windows = compress(echoes, jnp.asarray(range_tables()))
    turned = lax.all_to_all(windows, "pulse", split_axis=0, concat_axis=0, tiled=True)
    gain = window_gain(range_phase, band_lo, band_hi, block_index)
    rates = jnp.broadcast_to(azimuth_rate[:, None], (RB_DEV, LANES))
    filt, cos_p, sin_p, base, last_lanes, last_twiddle = prepare(
        scalars, rates, recon_filter.reshape(2 * CHANS * CHANS, PULSES)
    )
    doppler = spectra(
        turned, rows_table, jnp.asarray(lane_tables()), jnp.asarray(twiddle_tables()), gain
    )
    gathered = lax.all_to_all(doppler, "chan", split_axis=0, concat_axis=0, tiled=True)
    summed = merge(scalars, gathered, filt, cos_p, sin_p, base)
    combined = lax.all_to_all(summed, "chan", split_axis=0, concat_axis=0, tiled=True)
    return image(combined, rows_table, last_lanes, last_twiddle)


def solution(mesh):
    in_specs = (P(None, "chan", "pulse", None), P(), P("pulse"), P("pulse"), P("pulse"), P(), P())
    out_specs = P(None, "pulse", "chan")
    return jax.shard_map(
        per_device, mesh=mesh, in_specs=in_specs, out_specs=out_specs, check_vma=False
    )
```

profile of v0, /device:TPU:1, one launch (start us, length us, event | category | flops | bytes accessed | tf_op | source)
XLA Modules:
  0.0 68.3 jit_solution(5982407063342541229)
XLA Ops:
  0.0 0.0 copy-start
  0.0 1.6 %copy-done = bf16[4,256,1024]{2,1,0:T(8,128)(2,1)S(1)} copy-done((bf16[4,256,1024]{2,1,0:T(8,128)(2,1)S(1)}, bf16[4,256,1024]{2,1,0:T(8,128)(2,1)}, u32[]{:S(2)}) %copy-start) | copy-done | bytes 2097176
  1.6 0.0 copy-start.1
  1.6 1.2 %copy-done.1 = bf16[2,1,64,4096]{3,2,1,0:T(8,128)(2,1)S(1)} copy-done((bf16[2,1,64,4096]{3,2,1,0:T(8,128)(2,1)S(1)}, bf16[2,1,64,4096]{3,2,1,0:T(8,128)(2,1)}, u32[]{:S(2)}) %copy-start.1) | copy-done | bytes 1048600
  2.8 0.0 copy-start.6
  2.8 0.0 copy-start.2
  2.8 0.0 copy-start.3
  2.8 0.0 copy-start.4
  2.8 2.7 %compress.1 = bf16[64,8,384]{2,1,0:T(8,128)(2,1)} custom-call(bf16[2,1,64,4096]{3,2,1,0:T(8,128)(2,1)S(1)} %copy-done.1, bf16[4,256,1024]{2,1,0:T(8,128)(2,1)S(1)} %copy-done), custom_call_target="tpu_custom_call" | custom-call | flops 536870912 | bytes 4194304 | tf_op jit(solution)/shard_map/compress/pallas_call | solution.py:139
  5.6 17.3 %all-to-all-start = ((bf16[64,8,384]{2,1,0:T(8,128)(2,1)}), bf16[64,8,384]{2,1,0:T(8,128)(2,1)S(1)}, u32[]{:S(2)}, u32[]{:S(2)}) async-start(bf16[64,8,384]{2,1,0:T(8,128)(2,1)} %compress.1), calls=%async_computation | async-start | bytes 786432 | tf_op jit(solution)/shard_map/all_to_all | solution.py:424
  24.1 0.0 copy-done.6
  24.2 0.1 cosine_multiply_fusion
  24.3 0.1 stack.17
  24.4 0.1 stack.18
  24.5 13.4 %all-to-all-done.turned_ref = bf16[64,8,384]{2,1,0:T(8,128)(2,1)S(1)} async-done(((bf16[64,8,384]{2,1,0:T(8,128)(2,1)}), bf16[64,8,384]{2,1,0:T(8,128)(2,1)S(1)}, u32[]{:S(2)}, u32[]{:S(2)}) %all-to-all-start) | async-done | bytes 393248 | tf_op jit(solution)/shard_map/all_to_all | solution.py:424
  37.9 0.1 broadcast_in_dim.24.gain_ref
  37.9 0.0 copy-done.2
  37.9 0.0 copy-done.3
  37.9 0.0 copy-done.4
  38.0 2.6 %spectra.1 = bf16[8,96,256]{2,1,0:T(8,128)(2,1)} custom-call(bf16[64,8,384]{2,1,0:T(8,128)(2,1)S(1)} %all-to-all-done.turned_ref, bf16[1024,256]{1,0:T(8,128)(2,1)S(1)} %copy-done.2, bf16[256,512]{1,0:T(8,128)(2,1)S(1)} %copy-done.4, f32[256,256]{1,0:T(8,128)S(1)} %copy-done.3, f32[2,3,8,128]{3,2,1,0:T(8,128)S(1)} %broadcast_in_dim.24.gain_ref), custom_call_target="tpu_custom_call" | custom-call | flops 704643072 | bytes 2097152 | tf_op jit(solution)/shard_map/spectra/pallas_call | solution.py:190
  40.5 7.7 %all-to-all-start.1 = ((bf16[8,96,256]{2,1,0:T(8,128)(2,1)}), bf16[8,96,256]{2,1,0:T(8,128)(2,1)S(1)}, u32[]{:S(2)}, u32[]{:S(2)}) async-start(bf16[8,96,256]{2,1,0:T(8,128)(2,1)} %spectra.1), calls=%async_computation.1 | async-start | bytes 786432 | tf_op jit(solution)/shard_map/all_to_all | solution.py:433
  48.2 0.0 copy-done.5
  48.2 0.4 reshape.9.filter_ref
  48.7 0.0 copy-done.8
  48.7 0.1 pad_add_fusion.scalars
  48.7 0.0 copy-done.7
  48.7 0.1 broadcast_in_dim.25.rate_ref
  48.8 2.0 %prepare.1 = (f32[4,128,128]{2,1,0:T(8,128)S(1)}, f32[8,32,128]{2,1,0:T(8,128)S(1)}, f32[8,32,128]{2,1,0:T(8,128)S(1)}, f32[8,32,128]{2,1,0:T(8,128)S(1)}, bf16[...) custom-call(s32[10]{0:T(128)S(1)} %pad_add_fusion.scalars, f32[8,128]{1,0:T(8,128)S(1)} %broadcast_in_dim.25.rate_ref, ...), custom_call_target="tpu_custom_call" | custom-call | flops 536870912 | bytes 2097152 | tf_op jit(solution)/shard_map/prepare/pallas_call | solution.py:261
  50.8 5.5 %all-to-all-done.1.gathered_ref = bf16[8,96,256]{2,1,0:T(8,128)(2,1)S(1)} async-done(((bf16[8,96,256]{2,1,0:T(8,128)(2,1)}), bf16[8,96,256]{2,1,0:T(8,128)(2,1)S(1)}, u32[]{:S(2)}, u32[]{:S(2)}) %all-to-all-start.1) | async-done | bytes 393248 | tf_op jit(solution)/shard_map/all_to_all | solution.py:433
  56.3 2.1 %merge.1 = bf16[8,32,256]{2,1,0:T(8,128)(2,1)S(1)} custom-call(s32[10]{0:T(128)S(1)} %pad_add_fusion.scalars, bf16[8,96,256]{2,1,0:T(8,128)(2,1)S(1)} %all-to-all-done.1.gathered_ref, f32[4,128,128]{2,1,0:T(8,128)S(1)} %get-tuple-element.11.filt_ref, f32[8,32,128]{2,1,0:T(8,128)S(1)} %get-tuple-element.12.cos_ref, ...), custom_call_target="tpu_custom_call" | custom-call | flops 16777216 | bytes 2097152 | tf_op jit(solution)/shard_map/merge/pallas_call | solution.py:358
  58.4 8.5 %all_to_all.15.combined_ref = bf16[8,32,256]{2,1,0:T(8,128)(2,1)S(1)} all-to-all(bf16[8,32,256]{2,1,0:T(8,128)(2,1)S(1)} %merge.1), channel_id=1, replica_groups=mesh['pulse'=64,'chan'=8] {'chan'}, dimensions={0} | all-to-all | bytes 262144 | tf_op jit(solution)/shard_map/all_to_all | solution.py:435
  66.9 1.4 %image.1 = f32[2,8,4096]{2,1,0:T(8,128)} custom-call(bf16[8,32,256]{2,1,0:T(8,128)(2,1)S(1)} %all_to_all.15.combined_ref, bf16[1024,256]{1,0:T(8,128)(2,1)S(1)} %copy-done.2, bf16[256,512]{1,0:T(8,128)(2,1)S(1)} %get-tuple-element.15.lanes_ref, f32[256,256]{1,0:T(8,128)S(1)} %get-tuple-element.16.twiddle_ref), custom_call_target="tpu_custom_call" | custom-call | flops 268435456 | bytes 2097152 | tf_op jit(solution)/shard_map/image/pallas_call | solution.py:396
  (4 shorter events, 0.0 us)
Async XLA Ops:
  0.0 1.6 %copy-start = (bf16[4,256,1024]{2,1,0:T(8,128)(2,1)S(1)}, bf16[4,256,1024]{2,1,0:T(8,128)(2,1)}, u32[]{:S(2)}) copy-start(bf16[4,256,1024]{2,1,0:T(8,128)(2,1)} %constant.31.clone.table_ref) | copy-start | bytes 6291460
  1.6 1.2 %copy-start.1 = (bf16[2,1,64,4096]{3,2,1,0:T(8,128)(2,1)S(1)}, bf16[2,1,64,4096]{3,2,1,0:T(8,128)(2,1)}, u32[]{:S(2)}) copy-start(bf16[2,1,64,4096]{3,2,1,0:T(8,128)(2,1)} %echo_ref.1) | copy-start | bytes 3145732
  2.8 21.3 %copy-start.6 = (f32[512]{0:T(512)S(1)}, f32[512]{0:T(512)}, u32[]{:S(2)}) copy-start(f32[512]{0:T(512)} %param.12) | copy-start | bytes 6148
  2.8 35.1 %copy-start.2 = (bf16[1024,256]{1,0:T(8,128)(2,1)S(1)}, bf16[1024,256]{1,0:T(8,128)(2,1)}, u32[]{:S(2)}) copy-start(bf16[1024,256]{1,0:T(8,128)(2,1)} %constant.30.clone.rows_ref) | copy-start | bytes 1572868
  2.8 35.1 %copy-start.3 = (f32[256,256]{1,0:T(8,128)S(1)}, f32[256,256]{1,0:T(8,128)}, u32[]{:S(2)}) copy-start(f32[256,256]{1,0:T(8,128)} %constant.33.clone.twiddle_ref) | copy-start | bytes 786436
  2.8 35.1 %copy-start.4 = (bf16[256,512]{1,0:T(8,128)(2,1)S(1)}, bf16[256,512]{1,0:T(8,128)(2,1)}, u32[]{:S(2)}) copy-start(bf16[256,512]{1,0:T(8,128)(2,1)} %constant.32.clone.lanes_ref) | copy-start | bytes 786436
  5.6 42.7 %copy-start.5 = (bf16[8,8,2,4096]{3,2,1,0:T(2,128)(2,1)S(1)}, bf16[8,8,2,4096]{3,2,1,0:T(2,128)(2,1)}, u32[]{:S(2)}) copy-start(bf16[8,8,2,4096]{3,2,1,0:T(2,128)(2,1)} %param.17) | copy-start | bytes 3145732
  5.6 32.3 %all-to-all-start = ((bf16[64,8,384]{2,1,0:T(8,128)(2,1)}), bf16[64,8,384]{2,1,0:T(8,128)(2,1)S(1)}, u32[]{:S(2)}, u32[]{:S(2)}) async-start(bf16[64,8,384]{2,1,0:T(8,128)(2,1)} %compress.1), calls=%async_computation | async-start | bytes 786432 | tf_op jit(solution)/shard_map/all_to_all | solution.py:424
  40.5 8.1 %copy-start.8 = (s32[8]{0:T(128)S(1)}, s32[8]{0:T(128)}, u32[]{:S(2)}) copy-start(s32[8]{0:T(128)} %param.16) | copy-start | bytes 100
  40.5 8.2 %copy-start.7 = (f32[8]{0:T(128)S(1)}, f32[8]{0:T(128)}, u32[]{:S(2)}) copy-start(f32[8]{0:T(128)} %param.13) | copy-start | bytes 100
  40.5 15.8 %all-to-all-start.1 = ((bf16[8,96,256]{2,1,0:T(8,128)(2,1)}), bf16[8,96,256]{2,1,0:T(8,128)(2,1)S(1)}, u32[]{:S(2)}, u32[]{:S(2)}) async-start(bf16[8,96,256]{2,1,0:T(8,128)(2,1)} %spectra.1), calls=%async_computation.1 | async-start | bytes 786432 | tf_op jit(solution)/shard_map/all_to_all | solution.py:433
where the time goes:
time: 68.7 us; the launch traced here: 68.3 us
  starting transfers between devices  24.9 us (36%)
  waiting for transfers between devices  18.9 us (28%)
  Pallas kernels  10.8 us (16%)
  blocking collectives  8.53 us (12%)
  local copies, waits for them, and re-layouts  3.56 us (5%)
  between operations  1.37 us (2%)
    all_to_all x1, starting transfers between devices, per_device(): lax.all_to_all(windows, 'pulse', split_axis=0, concat_axis=0, tiled=True)  17.3 us
    all_to_all x1, waiting for transfers between devices, per_device(): lax.all_to_all(windows, 'pulse', split_axis=0, concat_axis=0, tiled=True)  13.4 us
    all_to_all x1, blocking collectives, per_device(): lax.all_to_all(summed, 'chan', split_axis=0, concat_axis=0, tiled=True)  8.53 us
    all_to_all x1, starting transfers between devices, per_device(): lax.all_to_all(doppler, 'chan', split_axis=0, concat_axis=0, tiled=True)  7.68 us
    all_to_all x1, waiting for transfers between devices, per_device(): lax.all_to_all(doppler, 'chan', split_axis=0, concat_axis=0, tiled=True)  5.53 us
    unnamed x18, local copies, waits for them, and re-layouts  2.84 us
    pallas_call x1, Pallas kernels, compress(): pl.pallas_call(compress_kernel, grid=(RADIX,), in_specs=[pl.BlockSpec((2,...  2.74 us
    pallas_call x1, Pallas kernels, spectra(): pl.pallas_call(spectra_kernel, out_shape=jax.ShapeDtypeStruct((CHANS, 96,...  2.59 us
  transfers between devices with their start and end apart: 2, of which 2 were waited for; matrix products, arithmetic and copies ran while one was open for 1% of the time, Pallas kernels for 3%

commit v1 on v0

v1 whole, which is shorter than its diff:
```python
import math

import jax
import jax.numpy as jnp
import numpy as np
from jax import lax
from jax.experimental import pallas as pl
from jax.experimental.pallas import tpu as pltpu
from jax.sharding import PartitionSpec as P

NS = 4096
RB_DEV = 8
MIGRATION = 7
PULSES = 4096
NR = 512
CHANS = 8
SPECTRUM = 32768
N_PULSE = 64

RADIX = 4
FOLD = NS // RADIX
LANES = 128
ROWS = PULSES // LANES
OWN = ROWS // CHANS
PULSES_DEV = PULSES // N_PULSE
curvature = 300.0

f32 = jnp.float32
bf16 = jnp.bfloat16


def split_np(values):
    high = np.asarray(values, np.float32).astype(bf16)
    low = (values - high.astype(np.float64)).astype(np.float32).astype(bf16)
    return high, low


def range_tables():
    tables = []
    sample = np.arange(FOLD)
    for rho in range(RADIX):
        bins = np.array([8 * block + 4 * h + rho for h in range(2) for block in range(N_PULSE)])
        angle = (bins[:, None] * sample[None, :]) % NS * (2.0 * math.pi / NS)
        tables.append(np.concatenate([np.cos(angle), np.sin(angle)], axis=0))
    return np.stack(tables).astype(np.float32).astype(bf16)


def lane_tables():
    digit = np.arange(LANES)
    angle = (digit[:, None] * digit[None, :]) % LANES * (2.0 * math.pi / LANES)
    cos_m, sin_m = np.cos(angle), np.sin(angle)
    high, low = split_np(np.block([[cos_m, -sin_m], [sin_m, cos_m]]))
    return np.concatenate([high, low], axis=1)


def twiddle_tables():
    angle = np.arange(ROWS)[:, None] * np.arange(LANES)[None, :] * (2.0 * math.pi / PULSES)
    angle = np.repeat(angle, RB_DEV, axis=0)
    return np.concatenate([np.cos(angle), np.sin(angle)], axis=1).astype(np.float32)


def dot(left, right):
    return jnp.dot(left, right, preferred_element_type=f32)


def split(values):
    high = values.astype(bf16)
    return high, (values - high.astype(f32)).astype(bf16)


def lane_index(shape):
    return lax.broadcasted_iota(jnp.int32, shape, 1)


def compress_kernel(echo_hbm, table_hbm, out_ref, echo, table, folded, bins, echo_sem, table_sem):
    def echo_copy(part):
        return pltpu.make_async_copy(echo_hbm.at[part, 0], echo.at[part], echo_sem.at[part])

    def table_copy(residue):
        return pltpu.make_async_copy(
            table_hbm.at[residue], table.at[residue], table_sem.at[residue]
        )

    for part in range(2):
        echo_copy(part).start()
    for residue in range(RADIX):
        table_copy(residue).start()
    for part in range(2):
        echo_copy(part).wait()

    def put(residue, part, rows, cols, values):
        high, low = split(values)
        folded[residue, part * 64 + rows : part * 64 + rows + 16, cols] = high
        folded[residue, 128 + part * 64 + rows : 128 + part * 64 + rows + 16, cols] = low

    width = 256
    for rows in range(0, PULSES_DEV, 16):
        for left in range(0, FOLD, width):
            cols = slice(left, left + width)
            pieces = [
                [
                    echo[part, rows : rows + 16, a * FOLD + left : a * FOLD + left + width].astype(f32)
                    for a in range(RADIX)
                ]
                for part in range(2)
            ]
            (re0, re1, re2, re3), (im0, im1, im2, im3) = pieces
            re_s, re_t, im_s, im_t = re0 + re2, re1 + re3, im0 + im2, im1 + im3
            put(0, 0, rows, cols, re_s + re_t)
            put(0, 1, rows, cols, im_s + im_t)
            put(2, 0, rows, cols, re_s - re_t)
            put(2, 1, rows, cols, im_s - im_t)
            re_s, re_t, im_s, im_t = re0 - re2, re1 - re3, im0 - im2, im1 - im3
            put(1, 0, rows, cols, re_s + im_t)
            put(1, 1, rows, cols, im_s - re_t)
            put(3, 0, rows, cols, re_s - im_t)
            put(3, 1, rows, cols, im_s + re_t)

    for residue in range(RADIX):
        table_copy(residue).wait()
    sign = jnp.where(lane_index((128, LANES)) < 64, 1.0, -1.0)
    for residue in range(RADIX):
        sums = lax.dot_general(
            table[residue], folded[residue], (((1,), (1,)), ((), ())), preferred_element_type=f32
        )
        sums = sums[:, :LANES] + sums[:, LANES:]
        comp = sums[:128] + sign * pltpu.roll(sums[128:], 64, 1)
        for h in range(2):
            bins[pl.ds(4 * h + residue, N_PULSE, stride=RB_DEV), :] = comp[
                h * N_PULSE : (h + 1) * N_PULSE
            ]
    own = bins[...].astype(bf16).reshape(N_PULSE, RB_DEV, LANES)
    edge = jnp.zeros((1, RB_DEV, LANES), bf16)
    out_ref[0:1, :, 0:LANES] = edge
    out_ref[1:N_PULSE, :, 0:LANES] = own[: N_PULSE - 1]
    out_ref[:, :, LANES : 2 * LANES] = own
    out_ref[0 : N_PULSE - 1, :, 2 * LANES :] = own[1:]
    out_ref[N_PULSE - 1 :, :, 2 * LANES :] = edge


def compress(echoes, tables):
    whole = pl.BlockSpec(memory_space=pl.ANY)
    return pl.pallas_call(
        compress_kernel,
        in_specs=[whole, whole],
        out_shape=jax.ShapeDtypeStruct((N_PULSE, RB_DEV, 3 * LANES), bf16),
        scratch_shapes=[
            pltpu.VMEM((2, PULSES_DEV, NS), bf16),
            pltpu.VMEM((RADIX, 256, FOLD), bf16),
            pltpu.VMEM((RADIX, 256, FOLD), bf16),
            pltpu.VMEM((NR, LANES), f32),
            pltpu.SemaphoreType.DMA((2,)),
            pltpu.SemaphoreType.DMA((RADIX,)),
        ],
        compiler_params=pltpu.CompilerParams(vmem_limit_bytes=60 << 20),
        cost_estimate=pl.CostEstimate(
            flops=2 * RADIX * 256 * 256 * FOLD, bytes_accessed=4 << 20, transcendentals=0
        ),
        name="compress",
    )(echoes, tables)


def add(u, v):
    return (u[0] + v[0], u[1] + v[1])


def sub(u, v):
    return (u[0] - v[0], u[1] - v[1])


def times_i(u):
    return (-u[1], u[0])


def turn(u, angle):
    cos_a, sin_a = math.cos(angle), math.sin(angle)
    return (u[0] * cos_a - u[1] * sin_a, u[1] * cos_a + u[0] * sin_a)


def fft4(v0, v1, v2, v3):
    e0, e1 = add(v0, v2), sub(v0, v2)
    o0, o1 = add(v1, v3), times_i(sub(v1, v3))
    return [add(e0, o0), add(e1, o1), sub(e0, o0), sub(e1, o1)]


def fft8(values):
    half = math.sqrt(0.5)
    even = fft4(values[0], values[2], values[4], values[6])
    odd = fft4(values[1], values[3], values[5], values[7])
    odd[1] = ((odd[1][0] - odd[1][1]) * half, (odd[1][0] + odd[1][1]) * half)
    odd[2] = times_i(odd[2])
    odd[3] = ((-odd[3][0] - odd[3][1]) * half, (odd[3][0] - odd[3][1]) * half)
    return [add(e, o) for e, o in zip(even, odd)] + [sub(e, o) for e, o in zip(even, odd)]


def fft32(load, hold, store):
    for v in range(4):
        firsts = fft8([load(4 * u + v) for u in range(8)])
        for t in range(8):
            value = firsts[t]
            if t * v:
                value = turn(value, 2.0 * math.pi * t * v / 32)
            hold[0, v * 8 + t] = value[0]
            hold[1, v * 8 + t] = value[1]
    for t in range(8):
        seconds = fft4(*[(hold[0, v * 8 + t], hold[1, v * 8 + t]) for v in range(4)])
        for s in range(4):
            store(8 * s + t, seconds[s])


def spectra_kernel(turned_ref, lanes_ref, twiddle_ref, out_ref, hold, samples):
    low_half = lane_index((RB_DEV, LANES)) < 64
    table_hi, table_lo = lanes_ref[:, :256], lanes_ref[:, 256:]
    for group in range(3):
        cols = slice(group * LANES, (group + 1) * LANES)

        def load(p_hi):
            even = turned_ref[2 * p_hi, :, cols].astype(f32)
            odd = turned_ref[2 * p_hi + 1, :, cols].astype(f32)
            real_x = jnp.where(low_half, even, pltpu.roll(odd, 64, 1))
            imag_x = jnp.where(low_half, pltpu.roll(even, 64, 1), odd)
            return (imag_x, real_x)

        def store(j_lo, value):
            imag_y, real_y = value
            rows = slice(j_lo * RB_DEV, (j_lo + 1) * RB_DEV)
            tw_re = twiddle_ref[group, rows, :LANES]
            tw_im = twiddle_ref[group, rows, LANES:]
            samples[group, rows, :LANES] = real_y * tw_re - imag_y * tw_im
            samples[group, rows, LANES:] = imag_y * tw_re + real_y * tw_im

        fft32(load, hold.at[group], store)
        high, low = split(samples[group])
        result = dot(high, table_hi) + (dot(low, table_hi) + dot(high, table_lo))
        out_ref[:, group * 32 : (group + 1) * 32, :] = result.astype(bf16).reshape(
            CHANS, 32, 256
        )


def spectra(turned, lanes_table, twiddle):
    return pl.pallas_call(
        spectra_kernel,
        out_shape=jax.ShapeDtypeStruct((CHANS, 96, 256), bf16),
        scratch_shapes=[
            pltpu.VMEM((3, 2, ROWS, RB_DEV, LANES), f32),
            pltpu.VMEM((3, 256, 256), f32),
        ],
        compiler_params=pltpu.CompilerParams(vmem_limit_bytes=32 << 20),
        cost_estimate=pl.CostEstimate(
            flops=6 * 256 * 256 * 768, bytes_accessed=2 << 20, transcendentals=0
        ),
        name="spectra",
    )(turned, lanes_table, twiddle)


def prepare_kernel(
    scalars,
    rate_ref,
    gain_ref,
    turns_ref,
    filter_ref,
    filt_ref,
    cos_ref,
    sin_ref,
    base_ref,
    lanes_ref,
    twiddle_ref,
    first_ref,
):
    chan = scalars[CHANS]
    block = scalars[CHANS + 1]
    tw_cos = turns_ref[:, :LANES].reshape(ROWS, RB_DEV, LANES)
    tw_sin = turns_ref[:, LANES:].reshape(ROWS, RB_DEV, LANES)
    for group in range(3):
        gain_re, gain_im = gain_ref[0, group][None], gain_ref[1, group][None]
        first_ref[group, :, :LANES] = (gain_re * tw_cos + gain_im * tw_sin).reshape(256, LANES)
        first_ref[group, :, LANES:] = (gain_im * tw_cos - gain_re * tw_sin).reshape(256, LANES)
    shape = (OWN * RB_DEV, LANES)
    row = lax.broadcasted_iota(jnp.int32, shape, 0)
    lane = lax.broadcasted_iota(jnp.int32, shape, 1)
    doppler_bin = 32 * lane + OWN * chan + lax.shift_right_logical(row, 3)
    q = jnp.bitwise_and(row, 7)
    bins = (block * RB_DEV + q).astype(f32)
    slope = 0.5 + 0.5 * bins / NR
    place = (RB_DEV + q).astype(f32)
    rates = jnp.concatenate([rate_ref[...]] * OWN, axis=0)
    for k in range(CHANS):
        doppler = (k * PULSES + doppler_bin).astype(f32) / SPECTRUM - 0.5
        spread = 2.0 * jnp.square(2.0 * doppler) * slope - 1.0
        base_ref[k] = place - (place + MIGRATION * spread)
        phase = -curvature * jnp.square(doppler) / rates
        cos_ref[k] = jnp.cos(phase)
        sin_ref[k] = jnp.sin(phase)
    pick_x = lax.broadcasted_iota(jnp.int32, (1024, LANES), 0)
    pick_y = lax.broadcasted_iota(jnp.int32, (1024, LANES), 1)
    wanted = 32 * jnp.bitwise_and(pick_y, 31) + OWN * chan + lax.shift_right_logical(pick_y, 5)
    pick = jnp.where(pick_x == wanted, 1.0, 0.0).astype(bf16)
    quarter = lax.shift_right_logical(lane_index((128, LANES)), 5)
    picked = [dot(filter_ref[:, 1024 * t : 1024 * (t + 1)], pick) for t in range(4)]
    for digit in range(OWN):
        total = jnp.zeros((128, LANES), f32)
        for t in range(4):
            moved = picked[t]
            if t != digit:
                moved = pltpu.roll(moved, (32 * (t - digit)) % LANES, 1)
            total = jnp.where(quarter == t, moved, total)
        filt_ref[digit] = total
    square = (LANES, LANES)
    j_hi = lax.broadcasted_iota(jnp.int32, square, 0)
    m_lo = lax.broadcasted_iota(jnp.int32, square, 1)
    turns = jnp.bitwise_and(8 * j_hi * m_lo + j_hi * chan, 1023)
    angle = turns.astype(f32) * (2.0 * math.pi / 1024)
    cos_hi, cos_lo = split(jnp.cos(angle))
    sin_hi, sin_lo = split(jnp.sin(angle))
    for at, (cos_m, sin_m) in enumerate(((cos_hi, sin_hi), (cos_lo, sin_lo))):
        left, mid, right = 256 * at, 256 * at + LANES, 256 * at + 256
        lanes_ref[:LANES, left:mid] = cos_m
        lanes_ref[:LANES, mid:right] = sin_m
        lanes_ref[LANES:, left:mid] = -sin_m
        lanes_ref[LANES:, mid:right] = cos_m
    small = (ROWS, LANES)
    j_lo = lax.broadcasted_iota(jnp.int32, small, 0)
    m_low = lax.broadcasted_iota(jnp.int32, small, 1)
    angle = (j_lo * (8 * m_low + chan)).astype(f32) * (2.0 * math.pi / SPECTRUM)
    scale = 1.0 / math.sqrt(SPECTRUM)
    for at, values in enumerate((jnp.cos(angle) * scale, jnp.sin(angle) * scale)):
        full = jnp.broadcast_to(values[:, None, :], (ROWS, RB_DEV, LANES)).reshape(256, LANES)
        twiddle_ref[:, at * LANES : (at + 1) * LANES] = full


def prepare(scalars, rates, gain, turns, filters):
    vmem = pl.BlockSpec(memory_space=pltpu.VMEM)
    return pl.pallas_call(
        prepare_kernel,
        in_specs=[pl.BlockSpec(memory_space=pltpu.SMEM)] + [vmem] * 4,
        out_shape=(
            jax.ShapeDtypeStruct((OWN, 128, LANES), f32),
            jax.ShapeDtypeStruct((CHANS, OWN * RB_DEV, LANES), f32),
            jax.ShapeDtypeStruct((CHANS, OWN * RB_DEV, LANES), f32),
            jax.ShapeDtypeStruct((CHANS, OWN * RB_DEV, LANES), f32),
            jax.ShapeDtypeStruct((256, 512), bf16),
            jax.ShapeDtypeStruct((256, 256), f32),
            jax.ShapeDtypeStruct((3, 256, 256), f32),
        ),
        compiler_params=pltpu.CompilerParams(vmem_limit_bytes=32 << 20),
        cost_estimate=pl.CostEstimate(
            flops=1 << 29, bytes_accessed=2 << 20, transcendentals=1 << 18
        ),
        name="prepare",
    )(scalars, rates, gain, turns, filters)


def band_steps(band):
    doppler = (band * PULSES + np.arange(PULSES)) / SPECTRUM - 0.5
    square = np.square(2.0 * doppler)
    lowest = MIGRATION * (2.0 * square.min() * 0.5 - 1.0) - 1e-3
    highest = MIGRATION * (2.0 * square.max() * (0.5 + 0.5 * (NR - 1) / NR) - 1.0) + 1e-3
    return range(max(-MIGRATION, math.floor(lowest)), min(MIGRATION, math.ceil(highest)) + 1)


def merge_kernel(
    scalars, gathered_ref, filt_ref, cos_ref, sin_ref, base_ref, out_ref, wide, merged, bands
):
    wide[...] = gathered_ref[...].astype(f32)
    for band in range(CHANS):
        steps = band_steps(band)
        groups = [1]
        if steps[0] < 0:
            groups = [0] + groups
        if steps[-1] > 0:
            groups = groups + [2]
        first_row = pl.multiple_of(scalars[CHANS + 2 + band] * 16, 16)
        for digit in range(OWN):
            rows = slice(digit * RB_DEV, (digit + 1) * RB_DEV)
            filters = filt_ref[digit, pl.ds(first_row, 16), :]
            sums_re = [None] * 3
            sums_im = [None] * 3
            for c in range(CHANS):
                f_re = jnp.broadcast_to(filters[2 * c : 2 * c + 1], (RB_DEV, LANES))
                f_im = jnp.broadcast_to(filters[2 * c + 1 : 2 * c + 2], (RB_DEV, LANES))
                for group in groups:
                    at = group * 32 + digit * RB_DEV
                    s_re = wide[c, at : at + RB_DEV, :LANES]
                    s_im = wide[c, at : at + RB_DEV, LANES:]
                    part_re = f_re * s_re - f_im * s_im
                    part_im = f_re * s_im + f_im * s_re
                    sums_re[group] = part_re if c == 0 else sums_re[group] + part_re
                    sums_im[group] = part_im if c == 0 else sums_im[group] + part_im
            slot = (band % 2) * OWN + digit
            for group in groups:
                span = slice(group * RB_DEV, (group + 1) * RB_DEV)
                merged[slot, 0, span, :] = sums_re[group]
                merged[slot, 1, span, :] = sums_im[group]
            base = base_ref[band, rows, :]
            moved_re = moved_im = None
            for step in steps:
                weight = jnp.maximum(0.0, 1.0 - jnp.abs(base + float(step)))
                first = RB_DEV + step
                part_re = weight * merged[slot, 0, first : first + RB_DEV, :]
                part_im = weight * merged[slot, 1, first : first + RB_DEV, :]
                moved_re = part_re if moved_re is None else moved_re + part_re
                moved_im = part_im if moved_im is None else moved_im + part_im
            cos_p = cos_ref[band, rows, :]
            sin_p = sin_ref[band, rows, :]
            bands[band, 0, rows, :] = moved_re * cos_p - moved_im * sin_p
            bands[band, 1, rows, :] = moved_im * cos_p + moved_re * sin_p
    for half in range(OWN * RB_DEV // 16):
        rows = slice(half * 16, half * 16 + 16)
        results = fft8([(bands[k, 0, rows, :], bands[k, 1, rows, :]) for k in range(CHANS)])
        for a in range(CHANS):
            out_ref[a, rows, :LANES] = results[a][0].astype(bf16)
            out_ref[a, rows, LANES:] = results[a][1].astype(bf16)


def merge(scalars, gathered, filt, cos_p, sin_p, base):
    vmem = pl.BlockSpec(memory_space=pltpu.VMEM)
    return pl.pallas_call(
        merge_kernel,
        in_specs=[pl.BlockSpec(memory_space=pltpu.SMEM)] + [vmem] * 5,
        out_shape=jax.ShapeDtypeStruct((CHANS, OWN * RB_DEV, 256), bf16),
        scratch_shapes=[
            pltpu.VMEM((CHANS, 96, 256), f32),
            pltpu.VMEM((2 * OWN, 2, 3 * RB_DEV, LANES), f32),
            pltpu.VMEM((CHANS, 2, OWN * RB_DEV, LANES), f32),
        ],
        compiler_params=pltpu.CompilerParams(vmem_limit_bytes=32 << 20),
        cost_estimate=pl.CostEstimate(flops=1 << 24, bytes_accessed=2 << 20, transcendentals=0),
        name="merge",
    )(scalars, gathered, filt, cos_p, sin_p, base)


def image_kernel(combined_ref, lanes_ref, twiddle_ref, out_ref, hold, samples):
    turned = dot(combined_ref[...].reshape(256, 256), lanes_ref[...])
    samples[...] = turned[:, :256] + turned[:, 256:]

    def load(j_lo):
        rows = slice(j_lo * RB_DEV, (j_lo + 1) * RB_DEV)
        real_y, imag_y = samples[rows, :LANES], samples[rows, LANES:]
        tw_cos, tw_sin = twiddle_ref[rows, :LANES], twiddle_ref[rows, LANES:]
        return (real_y * tw_cos - imag_y * tw_sin, imag_y * tw_cos + real_y * tw_sin)

    def store(m_hi, value):
        cols = slice(m_hi * LANES, (m_hi + 1) * LANES)
        out_ref[0, :, cols] = value[0]
        out_ref[1, :, cols] = value[1]

    fft32(load, hold, store)


def image(combined, lanes_table, twiddle):
    return pl.pallas_call(
        image_kernel,
        out_shape=jax.ShapeDtypeStruct((2, RB_DEV, PULSES), f32),
        scratch_shapes=[
            pltpu.VMEM((2, ROWS, RB_DEV, LANES), f32),
            pltpu.VMEM((256, 256), f32),
        ],
        compiler_params=pltpu.CompilerParams(vmem_limit_bytes=32 << 20),
        cost_estimate=pl.CostEstimate(
            flops=2 * 256 * 256 * 512, bytes_accessed=2 << 20, transcendentals=0
        ),
        name="image",
    )(combined, lanes_table, twiddle)


def window_gain(range_phase, band_lo, band_hi, block_index):
    slab_bins = block_index * RB_DEV - RB_DEV + lax.iota(jnp.int32, 3 * RB_DEV)
    inside = (slab_bins >= band_lo[0]) & (slab_bins < band_hi[0])
    scale = jnp.where(inside, 1.0 / math.sqrt(NS * PULSES), 0.0)
    phase = lax.dynamic_slice(
        jnp.pad(range_phase, (RB_DEV, RB_DEV)), (block_index * RB_DEV,), (3 * RB_DEV,)
    )
    gain = jnp.stack([scale * jnp.cos(phase), scale * jnp.sin(phase)])
    return jnp.broadcast_to(gain.reshape(2, 3, RB_DEV, 1), (2, 3, RB_DEV, LANES))


def per_device(echoes, range_phase, azimuth_rate, band_lo, band_hi, band_map, recon_filter):
    block_index = lax.axis_index("pulse").astype(jnp.int32)
    own_index = lax.axis_index("chan").astype(jnp.int32)
    order = lax.iota(jnp.int32, CHANS)
    row_of_band = jnp.sum(
        jnp.where(band_map[None, :] == order[:, None], order[None, :], 0), axis=1
    )
    scalars = jnp.concatenate([band_map, jnp.stack([own_index, block_index]), row_of_band])
    windows = compress(echoes, jnp.asarray(range_tables()))
    turned = lax.all_to_all(windows, "pulse", split_axis=0, concat_axis=0, tiled=True)
    gain = window_gain(range_phase, band_lo, band_hi, block_index)
    rates = jnp.broadcast_to(azimuth_rate[:, None], (RB_DEV, LANES))
    filt, cos_p, sin_p, base, last_lanes, last_twiddle, first_twiddle = prepare(
        scalars,
        rates,
        gain,
        jnp.asarray(twiddle_tables()),
        recon_filter.reshape(2 * CHANS * CHANS, PULSES),
    )
    doppler = spectra(turned, jnp.asarray(lane_tables()), first_twiddle)
    gathered = lax.all_to_all(doppler, "chan", split_axis=0, concat_axis=0, tiled=True)
    summed = merge(scalars, gathered, filt, cos_p, sin_p, base)
    combined = lax.all_to_all(summed, "chan", split_axis=0, concat_axis=0, tiled=True)
    return image(combined, last_lanes, last_twiddle)


def solution(mesh):
    in_specs = (P(None, "chan", "pulse", None), P(), P("pulse"), P("pulse"), P("pulse"), P(), P())
    out_specs = P(None, "pulse", "chan")
    return jax.shard_map(
        per_device, mesh=mesh, in_specs=in_specs, out_specs=out_specs, check_vma=False
    )
```

time: 68.7 us -> 63.7 us (0.927)
  blocking collectives: 8.53 us -> 23.9 us
  waiting for transfers between devices: 18.9 us -> 8.89 us
  starting transfers between devices: 24.9 us -> 17.1 us
  Pallas kernels: 10.8 us -> 9.31 us
  local copies, waits for them, and re-layouts: 3.56 us -> 2.37 us
    all_to_all x0 -> x1, blocking collectives: none -> 15.4 us  [per_device(): lax.all_to_all(doppler, 'chan', split_axis=0, concat_axis=0, tiled=True)]
    all_to_all x1 -> x0, starting transfers between devices: 7.68 us -> none  [per_device(): lax.all_to_all(doppler, 'chan', split_axis=0, concat_axis=0, tiled=True)]
    all_to_all x1 -> x0, waiting for transfers between devices: 5.53 us -> none  [per_device(): lax.all_to_all(doppler, 'chan', split_axis=0, concat_axis=0, tiled=True)]
    all_to_all x1, waiting for transfers between devices: 13.4 us -> 8.89 us  [per_device(): lax.all_to_all(windows, 'pulse', split_axis=0, concat_axis=0, tiled=True)]
    pallas_call x1, Pallas kernels: 2.59 us -> 0.79 us  [spectra(): pl.pallas_call(spectra_kernel, out_shape=jax.ShapeDtypeStruct((CHANS, 96,...]
    unnamed x18 -> x16, local copies, waits for them, and re-layouts: 2.84 us -> 1.64 us
    pallas_call x1, Pallas kernels: 2.74 us -> 3.83 us  [compress(): pl.pallas_call(compress_kernel, in_specs=[whole, whole], out_shape=jax.Sh...]
  transfers between devices with their start and end apart: 2 -> 1, of which waited for: 2 -> 1; matrix products, arithmetic and copies ran while one was open for 1% -> 2% of each run, Pallas kernels for 3% -> 3%
where the time goes in v1:
time: 63.7 us; the launch traced here: 63.4 us
  blocking collectives  23.9 us (38%)
  starting transfers between devices  17.1 us (27%)
  Pallas kernels  9.31 us (15%)
  waiting for transfers between devices  8.89 us (14%)
  local copies, waits for them, and re-layouts  2.37 us (4%)
  between operations  1.45 us (2%)
    all_to_all x1, starting transfers between devices, per_device(): lax.all_to_all(windows, 'pulse', split_axis=0, concat_axis=0, tiled=True)  17.1 us
    all_to_all x1, blocking collectives, per_device(): lax.all_to_all(doppler, 'chan', split_axis=0, concat_axis=0, tiled=True)  15.4 us
    all_to_all x1, waiting for transfers between devices, per_device(): lax.all_to_all(windows, 'pulse', split_axis=0, concat_axis=0, tiled=True)  8.89 us
    all_to_all x1, blocking collectives, per_device(): lax.all_to_all(summed, 'chan', split_axis=0, concat_axis=0, tiled=True)  8.52 us
    pallas_call x1, Pallas kernels, compress(): pl.pallas_call(compress_kernel, in_specs=[whole, whole], out_shape=jax.Sh...  3.83 us
    pallas_call x1, Pallas kernels, prepare(): pl.pallas_call(prepare_kernel, in_specs=[pl.BlockSpec(memory_space=pltpu....  2.06 us
    pallas_call x1, Pallas kernels, merge(): pl.pallas_call(merge_kernel, in_specs=[pl.BlockSpec(memory_space=pltpu.SM...  1.64 us
    unnamed x16, local copies, waits for them, and re-layouts  1.64 us
  transfers between devices with their start and end apart: 1, of which 1 were waited for; matrix products, arithmetic and copies ran while one was open for 2% of the time, Pallas kernels for 3%

profile of v1, /device:TPU:1, one launch (start us, length us, event | category | flops | bytes accessed | tf_op | source)
XLA Modules:
  0.0 63.4 jit_solution(17365324351562762135)
XLA Ops:
  0.0 0.0 copy-start.5
  0.0 0.0 copy-start.4
  0.0 3.8 %compress.1 = bf16[64,8,384]{2,1,0:T(8,128)(2,1)} custom-call(bf16[2,1,64,4096]{3,2,1,0:T(8,128)(2,1)} %echo_hbm.1, bf16[4,256,1024]{2,1,0:T(8,128)(2,1)} %constant.28.clone.table_hbm), custom_call_target="tpu_custom_call" | custom-call | flops 536870912 | bytes 4194304 | tf_op jit(solution)/shard_map/compress/pallas_call | solution.py:143
  3.8 0.0 copy-start.6
  3.9 0.0 copy-start.7
  3.9 17.1 %all-to-all-start = ((bf16[64,8,384]{2,1,0:T(8,128)(2,1)}), bf16[64,8,384]{2,1,0:T(8,128)(2,1)S(1)}, u32[]{:S(2)}, u32[]{:S(2)}) async-start(bf16[64,8,384]{2,1,0:T(8,128)(2,1)} %compress.1), calls=%async_computation | async-start | bytes 786432 | tf_op jit(solution)/shard_map/all_to_all | solution.py:486
  21.0 0.0 copy-start
  22.4 0.0 copy-done.5
  22.4 0.1 cosine_multiply_fusion
  22.5 0.1 stack.17
  22.6 0.1 stack.18
  22.7 0.0 copy-done.4
  22.7 0.4 reshape.10.filter_ref
  23.1 0.0 copy-done.6
  23.1 0.1 select_reduce_fusion
  23.2 0.1 pad_add_fusion.scalars
  23.3 0.1 broadcast_in_dim.42.gain_ref
  23.4 0.0 copy-done.7
  23.4 0.1 broadcast_in_dim.38.rate_ref
  23.5 0.0 copy-start.3
  23.5 1.0 %copy-done.3 = f32[256,256]{1,0:T(8,128)S(1)} copy-done((f32[256,256]{1,0:T(8,128)S(1)}, f32[256,256]{1,0:T(8,128)}, u32[]{:S(2)}) %copy-start.3) | copy-done | bytes 262168
  24.4 2.1 %prepare.1 = (f32[4,128,128]{2,1,0:T(8,128)S(1)}, f32[8,32,128]{2,1,0:T(8,128)S(1)}, f32[8,32,128]{2,1,0:T(8,128)S(1)}, f32[8,32,128]{2,1,0:T(8,128)S(1)}, bf16[...) custom-call(s32[18]{0:T(128)S(1)} %pad_add_fusion.scalars, ...), custom_call_target="tpu_custom_call" | custom-call | flops 536870912 | bytes 2097152 | tf_op jit(solution)/shard_map/prepare/pallas_call | solution.py:333
  26.5 0.0 copy-start.1
  26.5 0.6 %copy-done.1 = f32[8,32,128]{2,1,0:T(8,128)} copy-done((f32[8,32,128]{2,1,0:T(8,128)}, f32[8,32,128]{2,1,0:T(8,128)S(1)}, u32[]{:S(2)}) %copy-start.1) | copy-done | bytes 131096
  27.2 8.9 %all-to-all-done.turned_ref = bf16[64,8,384]{2,1,0:T(8,128)(2,1)S(1)} async-done(((bf16[64,8,384]{2,1,0:T(8,128)(2,1)}), bf16[64,8,384]{2,1,0:T(8,128)(2,1)S(1)}, u32[]{:S(2)}, u32[]{:S(2)}) %all-to-all-start) | async-done | bytes 393248 | tf_op jit(solution)/shard_map/all_to_all | solution.py:486
  36.0 0.0 copy-done
  36.1 0.8 %spectra.1 = bf16[8,96,256]{2,1,0:T(8,128)(2,1)S(1)} custom-call(bf16[64,8,384]{2,1,0:T(8,128)(2,1)S(1)} %all-to-all-done.turned_ref, bf16[256,512]{1,0:T(8,128)(2,1)S(1)} %copy-done, f32[3,256,256]{2,1,0:T(8,128)S(1)} %get-tuple-element.12.twiddle_ref), custom_call_target="tpu_custom_call" | custom-call | flops 301989888 | bytes 2097152 | tf_op jit(solution)/shard_map/spectra/pallas_call | solution.py:241
  36.8 15.4 %all_to_all.15.gathered_ref = bf16[8,96,256]{2,1,0:T(8,128)(2,1)S(1)} all-to-all(bf16[8,96,256]{2,1,0:T(8,128)(2,1)S(1)} %spectra.1), channel_id=1, replica_groups=mesh['pulse'=64,'chan'=8] {'chan'}, dimensions={0} | all-to-all | bytes 786432 | tf_op jit(solution)/shard_map/all_to_all | solution.py:497
  52.3 0.0 copy-done.2
  52.3 1.6 %merge.1 = bf16[8,32,256]{2,1,0:T(8,128)(2,1)S(1)} custom-call(s32[18]{0:T(128)S(1)} %pad_add_fusion.scalars, bf16[8,96,256]{2,1,0:T(8,128)(2,1)S(1)} %all_to_all.15.gathered_ref, f32[4,128,128]{2,1,0:T(8,128)S(1)} %get-tuple-element.13.filt_ref, f32[8,32,128]{2,1,0:T(8,128)S(1)} %get-tuple-element.14.cos_ref, f32[8,32,128]{2,1,0:T(8,128)S(1)} %get-tuple-element.15.sin_ref, ...), custom_call_target="tpu_custom_call" | custom-call | flops 16777216 | bytes 2097152 | tf_op jit(solution)/shard_map/merge/pallas_call | solution.py:417
  53.9 8.5 %all_to_all.16.combined_ref = bf16[8,32,256]{2,1,0:T(8,128)(2,1)S(1)} all-to-all(bf16[8,32,256]{2,1,0:T(8,128)(2,1)S(1)} %merge.1), channel_id=1, replica_groups=mesh['pulse'=64,'chan'=8] {'chan'}, dimensions={0} | all-to-all | bytes 262144 | tf_op jit(solution)/shard_map/all_to_all | solution.py:499
  62.4 1.0 %image.1 = f32[2,8,4096]{2,1,0:T(8,128)} custom-call(bf16[8,32,256]{2,1,0:T(8,128)(2,1)S(1)} %all_to_all.16.combined_ref, bf16[256,512]{1,0:T(8,128)(2,1)S(1)} %get-tuple-element.17.lanes_ref, f32[256,256]{1,0:T(8,128)S(1)} %get-tuple-element.18.twiddle_ref), custom_call_target="tpu_custom_call" | custom-call | flops 67108864 | bytes 2097152 | tf_op jit(solution)/shard_map/image/pallas_call | solution.py:451
  (2 shorter events, 0.0 us)
Async XLA Ops:
  0.0 22.4 %copy-start.5 = (f32[512]{0:T(512)S(1)}, f32[512]{0:T(512)}, u32[]{:S(2)}) copy-start(f32[512]{0:T(512)} %param.11) | copy-start | bytes 6148
  0.0 22.7 %copy-start.4 = (bf16[8,8,2,4096]{3,2,1,0:T(2,128)(2,1)S(1)}, bf16[8,8,2,4096]{3,2,1,0:T(2,128)(2,1)}, u32[]{:S(2)}) copy-start(bf16[8,8,2,4096]{3,2,1,0:T(2,128)(2,1)} %param.16) | copy-start | bytes 3145732
  3.8 19.3 %copy-start.6 = (s32[8]{0:T(128)S(1)}, s32[8]{0:T(128)}, u32[]{:S(2)}) copy-start(s32[8]{0:T(128)} %param.15) | copy-start | bytes 100
  3.9 19.6 %copy-start.7 = (f32[8]{0:T(128)S(1)}, f32[8]{0:T(128)}, u32[]{:S(2)}) copy-start(f32[8]{0:T(128)} %param.12) | copy-start | bytes 100
  3.9 32.2 %all-to-all-start = ((bf16[64,8,384]{2,1,0:T(8,128)(2,1)}), bf16[64,8,384]{2,1,0:T(8,128)(2,1)S(1)}, u32[]{:S(2)}, u32[]{:S(2)}) async-start(bf16[64,8,384]{2,1,0:T(8,128)(2,1)} %compress.1), calls=%async_computation | async-start | bytes 786432 | tf_op jit(solution)/shard_map/all_to_all | solution.py:486
  21.0 15.0 %copy-start = (bf16[256,512]{1,0:T(8,128)(2,1)S(1)}, bf16[256,512]{1,0:T(8,128)(2,1)}, u32[]{:S(2)}) copy-start(bf16[256,512]{1,0:T(8,128)(2,1)} %constant.30.clone.lanes_ref) | copy-start | bytes 786436
  23.5 1.0 %copy-start.3 = (f32[256,256]{1,0:T(8,128)S(1)}, f32[256,256]{1,0:T(8,128)}, u32[]{:S(2)}) copy-start(f32[256,256]{1,0:T(8,128)} %constant.29.clone.turns_ref) | copy-start | bytes 786436
  26.5 0.7 %copy-start.1 = (f32[8,32,128]{2,1,0:T(8,128)}, f32[8,32,128]{2,1,0:T(8,128)S(1)}, u32[]{:S(2)}) copy-start(f32[8,32,128]{2,1,0:T(8,128)S(1)} %get-tuple-element.16.base_ref) | copy-start | bytes 393220
  36.0 16.2 %copy-start.2 = (f32[8,32,128]{2,1,0:T(8,128)S(1)}, f32[8,32,128]{2,1,0:T(8,128)}, u32[]{:S(2)}) copy-start(f32[8,32,128]{2,1,0:T(8,128)} %copy-done.1) | copy-start | bytes 393220

commit v2 on v1

--- a/solution.py
+++ b/solution.py
@@ -21,7 +21,9 @@
 FOLD = NS // RADIX
 LANES = 128
 ROWS = PULSES // LANES
-OWN = ROWS // CHANS
+PAIR = 2
+OWN = ROWS // (PAIR * CHANS)
+OUT_ROWS = PAIR * RB_DEV * OWN
 PULSES_DEV = PULSES // N_PULSE
 curvature = 300.0
 
@@ -72,7 +74,18 @@
     return lax.broadcasted_iota(jnp.int32, shape, 1)
 
 
-def compress_kernel(echo_hbm, table_hbm, out_ref, echo, table, folded, bins, echo_sem, table_sem):
+def compress_kernel(
+    echo_hbm,
+    table_hbm,
+    out_ref,
+    zero_ref,
+    echo,
+    table,
+    folded,
+    bins,
+    echo_sem,
+    table_sem,
+):
     def echo_copy(part):
         return pltpu.make_async_copy(echo_hbm.at[part, 0], echo.at[part], echo_sem.at[part])
 
@@ -118,6 +131,7 @@
 
     for residue in range(RADIX):
         table_copy(residue).wait()
+    zero_ref[...] = jnp.zeros((RB_DEV, LANES), f32)
     sign = jnp.where(lane_index((128, LANES)) < 64, 1.0, -1.0)
     for residue in range(RADIX):
         sums = lax.dot_general(
@@ -129,21 +143,26 @@
             bins[pl.ds(4 * h + residue, N_PULSE, stride=RB_DEV), :] = comp[
                 h * N_PULSE : (h + 1) * N_PULSE
             ]
-    own = bins[...].astype(bf16).reshape(N_PULSE, RB_DEV, LANES)
+    own = bins[...].astype(bf16).reshape(N_PULSE // 2, 2, RB_DEV, LANES)
+    even, odd = own[:, 0], own[:, 1]
     edge = jnp.zeros((1, RB_DEV, LANES), bf16)
-    out_ref[0:1, :, 0:LANES] = edge
-    out_ref[1:N_PULSE, :, 0:LANES] = own[: N_PULSE - 1]
-    out_ref[:, :, LANES : 2 * LANES] = own
-    out_ref[0 : N_PULSE - 1, :, 2 * LANES :] = own[1:]
-    out_ref[N_PULSE - 1 :, :, 2 * LANES :] = edge
+    last = N_PULSE // 2 - 1
+    out_ref[0:1, 0, :, :LANES] = edge
+    out_ref[1:, 0, :, :LANES] = odd[:last]
+    out_ref[:, 0, :, LANES:] = even
+    out_ref[:, 1, :, :LANES] = odd
+    out_ref[:last, 1, :, LANES:] = even[1:]
+    out_ref[last:, 1, :, LANES:] = edge
 
 
 def compress(echoes, tables):
-    whole = pl.BlockSpec(memory_space=pl.ANY)
-    return pl.pallas_call(
+    windows, zeros = pl.pallas_call(
         compress_kernel,
-        in_specs=[whole, whole],
-        out_shape=jax.ShapeDtypeStruct((N_PULSE, RB_DEV, 3 * LANES), bf16),
+        in_specs=[pl.BlockSpec(memory_space=pl.ANY)] * 2,
+        out_shape=(
+            jax.ShapeDtypeStruct((N_PULSE // 2, 2, RB_DEV, 2 * LANES), bf16),
+            jax.ShapeDtypeStruct((RB_DEV, LANES), f32),
+        ),
         scratch_shapes=[
             pltpu.VMEM((2, PULSES_DEV, NS), bf16),
             pltpu.VMEM((RADIX, 256, FOLD), bf16),
@@ -158,6 +177,7 @@
         ),
         name="compress",
     )(echoes, tables)
+    return windows.reshape(N_PULSE, RB_DEV, 2 * LANES), zeros
 
 
 def add(u, v):
@@ -208,10 +228,11 @@
             store(8 * s + t, seconds[s])
 
 
-def spectra_kernel(turned_ref, lanes_ref, twiddle_ref, out_ref, hold, samples):
+def spectra_kernel(turned_ref, lanes_ref, twiddle_ref, after_ref, out_ref, hold, samples):
+    del after_ref
     low_half = lane_index((RB_DEV, LANES)) < 64
     table_hi, table_lo = lanes_ref[:, :256], lanes_ref[:, 256:]
-    for group in range(3):
+    for group in range(2):
         cols = slice(group * LANES, (group + 1) * LANES)
 
         def load(p_hi):
@@ -232,79 +253,77 @@
         fft32(load, hold.at[group], store)
         high, low = split(samples[group])
         result = dot(high, table_hi) + (dot(low, table_hi) + dot(high, table_lo))
-        out_ref[:, group * 32 : (group + 1) * 32, :] = result.astype(bf16).reshape(
-            CHANS, 32, 256
+        out_ref[:, group * 16 : (group + 1) * 16, :] = result.astype(bf16).reshape(
+            PAIR * CHANS, 16, 256
         )
 
 
-def spectra(turned, lanes_table, twiddle):
+def spectra(turned, lanes_table, twiddle, after):
+    vmem = pl.BlockSpec(memory_space=pltpu.VMEM)
     return pl.pallas_call(
         spectra_kernel,
-        out_shape=jax.ShapeDtypeStruct((CHANS, 96, 256), bf16),
+        in_specs=[vmem] * 3 + [pl.BlockSpec(memory_space=pl.ANY)],
+        out_shape=jax.ShapeDtypeStruct((PAIR * CHANS, 32, 256), bf16),
         scratch_shapes=[
-            pltpu.VMEM((3, 2, ROWS, RB_DEV, LANES), f32),
-            pltpu.VMEM((3, 256, 256), f32),
+            pltpu.VMEM((2, 2, ROWS, RB_DEV, LANES), f32),
+            pltpu.VMEM((2, 256, 256), f32),
         ],
         compiler_params=pltpu.CompilerParams(vmem_limit_bytes=32 << 20),
         cost_estimate=pl.CostEstimate(
-            flops=6 * 256 * 256 * 768, bytes_accessed=2 << 20, transcendentals=0
+            flops=4 * 256 * 256 * 768, bytes_accessed=2 << 20, transcendentals=0
         ),
         name="spectra",
-    )(turned, lanes_table, twiddle)
-
-
-def prepare_kernel(
+    )(turned, lanes_table, twiddle, after)
+
+
+def doppler_rows(scalars):
+    block = scalars[CHANS + 1]
+    member = jnp.bitwise_and(block, 1)
+    shape = (OUT_ROWS, LANES)
+    row = lax.broadcasted_iota(jnp.int32, shape, 0)
+    lane = lax.broadcasted_iota(jnp.int32, shape, 1)
+    digit = OWN * (member * CHANS + scalars[CHANS]) + lax.shift_right_logical(row, 4)
+    bins = (block - member) * RB_DEV + jnp.bitwise_and(row, 15)
+    return 32 * lane + digit, bins.astype(f32), jnp.bitwise_and(row, 7).astype(f32)
+
+
+def doppler_of(band, doppler_bin):
+    return (band * PULSES + doppler_bin).astype(f32) / SPECTRUM - 0.5
+
+
+def tables_kernel(
     scalars,
-    rate_ref,
     gain_ref,
     turns_ref,
     filter_ref,
     filt_ref,
-    cos_ref,
-    sin_ref,
-    base_ref,
     lanes_ref,
     twiddle_ref,
+    base_ref,
     first_ref,
 ):
     chan = scalars[CHANS]
-    block = scalars[CHANS + 1]
+    first_digit = OWN * (jnp.bitwise_and(scalars[CHANS + 1], 1) * CHANS + chan)
     tw_cos = turns_ref[:, :LANES].reshape(ROWS, RB_DEV, LANES)
     tw_sin = turns_ref[:, LANES:].reshape(ROWS, RB_DEV, LANES)
-    for group in range(3):
+    for group in range(2):
         gain_re, gain_im = gain_ref[0, group][None], gain_ref[1, group][None]
         first_ref[group, :, :LANES] = (gain_re * tw_cos + gain_im * tw_sin).reshape(256, LANES)
         first_ref[group, :, LANES:] = (gain_im * tw_cos - gain_re * tw_sin).reshape(256, LANES)
-    shape = (OWN * RB_DEV, LANES)
-    row = lax.broadcasted_iota(jnp.int32, shape, 0)
-    lane = lax.broadcasted_iota(jnp.int32, shape, 1)
-    doppler_bin = 32 * lane + OWN * chan + lax.shift_right_logical(row, 3)
-    q = jnp.bitwise_and(row, 7)
-    bins = (block * RB_DEV + q).astype(f32)
+    doppler_bin, bins, q = doppler_rows(scalars)
     slope = 0.5 + 0.5 * bins / NR
-    place = (RB_DEV + q).astype(f32)
-    rates = jnp.concatenate([rate_ref[...]] * OWN, axis=0)
+    place = RB_DEV + q
     for k in range(CHANS):
-        doppler = (k * PULSES + doppler_bin).astype(f32) / SPECTRUM - 0.5
-        spread = 2.0 * jnp.square(2.0 * doppler) * slope - 1.0
+        spread = 2.0 * jnp.square(2.0 * doppler_of(k, doppler_bin)) * slope - 1.0
         base_ref[k] = place - (place + MIGRATION * spread)
-        phase = -curvature * jnp.square(doppler) / rates
-        cos_ref[k] = jnp.cos(phase)
-        sin_ref[k] = jnp.sin(phase)
-    pick_x = lax.broadcasted_iota(jnp.int32, (1024, LANES), 0)
-    pick_y = lax.broadcasted_iota(jnp.int32, (1024, LANES), 1)
-    wanted = 32 * jnp.bitwise_and(pick_y, 31) + OWN * chan + lax.shift_right_logical(pick_y, 5)
+    pick_x = lax.broadcasted_iota(jnp.int32, (2048, LANES), 0)
+    pick_y = lax.broadcasted_iota(jnp.int32, (2048, LANES), 1)
+    wanted = 32 * jnp.bitwise_and(pick_y, 63) + first_digit + lax.shift_right_logical(pick_y, 6)
     pick = jnp.where(pick_x == wanted, 1.0, 0.0).astype(bf16)
-    quarter = lax.shift_right_logical(lane_index((128, LANES)), 5)
-    picked = [dot(filter_ref[:, 1024 * t : 1024 * (t + 1)], pick) for t in range(4)]
-    for digit in range(OWN):
-        total = jnp.zeros((128, LANES), f32)
-        for t in range(4):
-            moved = picked[t]
-            if t != digit:
-                moved = pltpu.roll(moved, (32 * (t - digit)) % LANES, 1)
-            total = jnp.where(quarter == t, moved, total)
-        filt_ref[digit] = total
+    low_half = lane_index((128, LANES)) < 64
+    left, right = [dot(filter_ref[:, 2048 * t : 2048 * (t + 1)], pick) for t in range(2)]
+    filt_ref[0] = jnp.where(low_half, left, pltpu.roll(right, 64, 1))
+    filt_ref[1] = jnp.where(low_half, pltpu.roll(left, 64, 1), right)
     square = (LANES, LANES)
     j_hi = lax.broadcasted_iota(jnp.int32, square, 0)
     m_lo = lax.broadcasted_iota(jnp.int32, square, 1)
@@ -328,26 +347,67 @@
         twiddle_ref[:, at * LANES : (at + 1) * LANES] = full
 
 
-def prepare(scalars, rates, gain, turns, filters):
+def tables(scalars, gain, turns, filters):
     vmem = pl.BlockSpec(memory_space=pltpu.VMEM)
     return pl.pallas_call(
-        prepare_kernel,
-        in_specs=[pl.BlockSpec(memory_space=pltpu.SMEM)] + [vmem] * 4,
+        tables_kernel,
+        in_specs=[pl.BlockSpec(memory_space=pltpu.SMEM)] + [vmem] * 3,
         out_shape=(
             jax.ShapeDtypeStruct((OWN, 128, LANES), f32),
-            jax.ShapeDtypeStruct((CHANS, OWN * RB_DEV, LANES), f32),
-            jax.ShapeDtypeStruct((CHANS, OWN * RB_DEV, LANES), f32),
-            jax.ShapeDtypeStruct((CHANS, OWN * RB_DEV, LANES), f32),
             jax.ShapeDtypeStruct((256, 512), bf16),
             jax.ShapeDtypeStruct((256, 256), f32),
-            jax.ShapeDtypeStruct((3, 256, 256), f32),
+            jax.ShapeDtypeStruct((CHANS, OUT_ROWS, LANES), f32),
+            jax.ShapeDtypeStruct((2, 256, 256), f32),
         ),
         compiler_params=pltpu.CompilerParams(vmem_limit_bytes=32 << 20),
         cost_estimate=pl.CostEstimate(
-            flops=1 << 29, bytes_accessed=2 << 20, transcendentals=1 << 18
-        ),
-        name="prepare",
-    )(scalars, rates, gain, turns, filters)
+            flops=1 << 28, bytes_accessed=2 << 20, transcendentals=1 << 16
+        ),
+        name="tables",
+    )(scalars, gain, turns, filters)
+
+
+def phases_kernel(scalars, own_ref, other_ref, cos_ref, sin_ref, mask_ref):
+    block = scalars[CHANS + 1]
+    member = jnp.bitwise_and(block, 1)
+    pair_start = (block - member) * RB_DEV
+    own, other = own_ref[...], other_ref[...]
+    given = [jnp.where(member == h, own, other) for h in range(PAIR)]
+    shape = (RB_DEV, LANES)
+    row = lax.broadcasted_iota(jnp.int32, shape, 0)
+    for h in range(PAIR):
+        low = jnp.broadcast_to(given[h][:, 64:65], shape)
+        high = jnp.broadcast_to(given[h][:, 96:97], shape)
+        for group in range(3):
+            bins = (pair_start + (h + group - 1) * RB_DEV + row).astype(f32)
+            inside = jnp.where(bins >= low, 1.0, 0.0) * jnp.where(bins < high, 1.0, 0.0)
+            mask_ref[h, group] = inside
+    doppler_bin = doppler_rows(scalars)[0]
+    rates = [jnp.broadcast_to(given[h][:, 0:1], (RB_DEV, LANES)) for h in range(PAIR)]
+    rates = jnp.concatenate(rates * OWN, axis=0)
+    for k in range(CHANS):
+        phase = -curvature * jnp.square(doppler_of(k, doppler_bin)) / rates
+        cos_ref[k] = jnp.cos(phase)
+        sin_ref[k] = jnp.sin(phase)
+
+
+def phases(scalars, own, other):
+    vmem = pl.BlockSpec(memory_space=pltpu.VMEM)
+    rows = jax.ShapeDtypeStruct((CHANS, OUT_ROWS, LANES), f32)
+    return pl.pallas_call(
+        phases_kernel,
+        in_specs=[pl.BlockSpec(memory_space=pltpu.SMEM)] + [vmem] * 2,
+        out_shape=(
+            rows,
+            rows,
+            jax.ShapeDtypeStruct((PAIR, 3, RB_DEV, LANES), f32),
+        ),
+        compiler_params=pltpu.CompilerParams(vmem_limit_bytes=32 << 20),
+        cost_estimate=pl.CostEstimate(
+            flops=1 << 24, bytes_accessed=1 << 20, transcendentals=1 << 18
+        ),
+        name="phases",
+    )(scalars, own, other)
 
 
 def band_steps(band):
@@ -359,74 +419,85 @@
 
 
 def merge_kernel(
-    scalars, gathered_ref, filt_ref, cos_ref, sin_ref, base_ref, out_ref, wide, merged, bands
+    scalars,
+    gathered_ref,
+    filt_ref,
+    cos_ref,
+    sin_ref,
+    base_ref,
+    mask_ref,
+    out_ref,
+    wide,
+    merged,
+    bands,
 ):
     wide[...] = gathered_ref[...].astype(f32)
     for band in range(CHANS):
         steps = band_steps(band)
-        groups = [1]
-        if steps[0] < 0:
-            groups = [0] + groups
-        if steps[-1] > 0:
-            groups = groups + [2]
+        reach = [group for group, used in ((0, steps[0] < 0), (1, True), (2, steps[-1] > 0)) if used]
+        needed = sorted({h + group for h in range(PAIR) for group in reach})
         first_row = pl.multiple_of(scalars[CHANS + 2 + band] * 16, 16)
         for digit in range(OWN):
-            rows = slice(digit * RB_DEV, (digit + 1) * RB_DEV)
             filters = filt_ref[digit, pl.ds(first_row, 16), :]
-            sums_re = [None] * 3
-            sums_im = [None] * 3
+            sums_re = [None] * 4
+            sums_im = [None] * 4
             for c in range(CHANS):
                 f_re = jnp.broadcast_to(filters[2 * c : 2 * c + 1], (RB_DEV, LANES))
                 f_im = jnp.broadcast_to(filters[2 * c + 1 : 2 * c + 2], (RB_DEV, LANES))
-                for group in groups:
-                    at = group * 32 + digit * RB_DEV
-                    s_re = wide[c, at : at + RB_DEV, :LANES]
-                    s_im = wide[c, at : at + RB_DEV, LANES:]
+                for part in needed:
+                    source = (part // 2) * CHANS + c
+                    at = (part % 2) * 16 + digit * RB_DEV
+                    s_re = wide[source, at : at + RB_DEV, :LANES]
+                    s_im = wide[source, at : at + RB_DEV, LANES:]
                     part_re = f_re * s_re - f_im * s_im
                     part_im = f_re * s_im + f_im * s_re
-                    sums_re[group] = part_re if c == 0 else sums_re[group] + part_re
-                    sums_im[group] = part_im if c == 0 else sums_im[group] + part_im
-            slot = (band % 2) * OWN + digit
-            for group in groups:
-                span = slice(group * RB_DEV, (group + 1) * RB_DEV)
-                merged[slot, 0, span, :] = sums_re[group]
-                merged[slot, 1, span, :] = sums_im[group]
-            base = base_ref[band, rows, :]
-            moved_re = moved_im = None
-            for step in steps:
-                weight = jnp.maximum(0.0, 1.0 - jnp.abs(base + float(step)))
-                first = RB_DEV + step
-                part_re = weight * merged[slot, 0, first : first + RB_DEV, :]
-                part_im = weight * merged[slot, 1, first : first + RB_DEV, :]
-                moved_re = part_re if moved_re is None else moved_re + part_re
-                moved_im = part_im if moved_im is None else moved_im + part_im
-            cos_p = cos_ref[band, rows, :]
-            sin_p = sin_ref[band, rows, :]
-            bands[band, 0, rows, :] = moved_re * cos_p - moved_im * sin_p
-            bands[band, 1, rows, :] = moved_im * cos_p + moved_re * sin_p
-    for half in range(OWN * RB_DEV // 16):
-        rows = slice(half * 16, half * 16 + 16)
-        results = fft8([(bands[k, 0, rows, :], bands[k, 1, rows, :]) for k in range(CHANS)])
+                    sums_re[part] = part_re if c == 0 else sums_re[part] + part_re
+                    sums_im[part] = part_im if c == 0 else sums_im[part] + part_im
+            for h in range(PAIR):
+                slot = ((band % 2) * OWN + digit) * PAIR + h
+                for group in reach:
+                    span = slice(group * RB_DEV, (group + 1) * RB_DEV)
+                    inside = mask_ref[h, group]
+                    merged[slot, 0, span, :] = sums_re[h + group] * inside
+                    merged[slot, 1, span, :] = sums_im[h + group] * inside
+                at = digit * PAIR * RB_DEV + h * RB_DEV
+                rows = slice(at, at + RB_DEV)
+                base = base_ref[band, rows, :]
+                moved_re = moved_im = None
+                for step in steps:
+                    weight = jnp.maximum(0.0, 1.0 - jnp.abs(base + float(step)))
+                    first = RB_DEV + step
+                    part_re = weight * merged[slot, 0, first : first + RB_DEV, :]
+                    part_im = weight * merged[slot, 1, first : first + RB_DEV, :]
+                    moved_re = part_re if moved_re is None else moved_re + part_re
+                    moved_im = part_im if moved_im is None else moved_im + part_im
+                cos_p = cos_ref[band, rows, :]
+                sin_p = sin_ref[band, rows, :]
+                to = slice(digit * RB_DEV, (digit + 1) * RB_DEV)
+                bands[band, 0, h, to, :] = moved_re * cos_p - moved_im * sin_p
+                bands[band, 1, h, to, :] = moved_im * cos_p + moved_re * sin_p
+    for h in range(PAIR):
+        results = fft8([(bands[k, 0, h], bands[k, 1, h]) for k in range(CHANS)])
         for a in range(CHANS):
-            out_ref[a, rows, :LANES] = results[a][0].astype(bf16)
-            out_ref[a, rows, LANES:] = results[a][1].astype(bf16)
-
-
-def merge(scalars, gathered, filt, cos_p, sin_p, base):
+            out_ref[h * CHANS + a, :, :LANES] = results[a][0].astype(bf16)
+            out_ref[h * CHANS + a, :, LANES:] = results[a][1].astype(bf16)
+
+
+def merge(scalars, gathered, filt, cos_p, sin_p, base, mask):
     vmem = pl.BlockSpec(memory_space=pltpu.VMEM)
     return pl.pallas_call(
         merge_kernel,
-        in_specs=[pl.BlockSpec(memory_space=pltpu.SMEM)] + [vmem] * 5,
-        out_shape=jax.ShapeDtypeStruct((CHANS, OWN * RB_DEV, 256), bf16),
+        in_specs=[pl.BlockSpec(memory_space=pltpu.SMEM)] + [vmem] * 6,
+        out_shape=jax.ShapeDtypeStruct((PAIR * CHANS, OWN * RB_DEV, 256), bf16),
         scratch_shapes=[
-            pltpu.VMEM((CHANS, 96, 256), f32),
-            pltpu.VMEM((2 * OWN, 2, 3 * RB_DEV, LANES), f32),
-            pltpu.VMEM((CHANS, 2, OWN * RB_DEV, LANES), f32),
+            pltpu.VMEM((PAIR * CHANS, 32, 256), f32),
+            pltpu.VMEM((2 * OWN * PAIR, 2, 3 * RB_DEV, LANES), f32),
+            pltpu.VMEM((CHANS, 2, PAIR, OWN * RB_DEV, LANES), f32),
         ],
         compiler_params=pltpu.CompilerParams(vmem_limit_bytes=32 << 20),
         cost_estimate=pl.CostEstimate(flops=1 << 24, bytes_accessed=2 << 20, transcendentals=0),
         name="merge",
-    )(scalars, gathered, filt, cos_p, sin_p, base)
+    )(scalars, gathered, filt, cos_p, sin_p, base, mask)
 
 
 def image_kernel(combined_ref, lanes_ref, twiddle_ref, out_ref, hold, samples):
@@ -463,15 +534,23 @@
     )(combined, lanes_table, twiddle)
 
 
-def window_gain(range_phase, band_lo, band_hi, block_index):
-    slab_bins = block_index * RB_DEV - RB_DEV + lax.iota(jnp.int32, 3 * RB_DEV)
-    inside = (slab_bins >= band_lo[0]) & (slab_bins < band_hi[0])
-    scale = jnp.where(inside, 1.0 / math.sqrt(NS * PULSES), 0.0)
-    phase = lax.dynamic_slice(
-        jnp.pad(range_phase, (RB_DEV, RB_DEV)), (block_index * RB_DEV,), (3 * RB_DEV,)
+def window_gain(range_phase, first_bin):
+    padded = jnp.pad(range_phase, (RB_DEV, RB_DEV))
+    phase = lax.dynamic_slice(padded, (first_bin + RB_DEV,), (2 * RB_DEV,))
+    scale = 1.0 / math.sqrt(NS * PULSES)
+    gain = jnp.stack([scale * jnp.cos(phase), scale * jnp.sin(phase)])
+    return jnp.broadcast_to(gain.reshape(2, 2, RB_DEV, 1), (2, 2, RB_DEV, LANES))
+
+
+def block_values(azimuth_rate, band_lo, band_hi):
+    return jnp.concatenate(
+        [
+            jnp.broadcast_to(azimuth_rate[:, None], (RB_DEV, 64)),
+            jnp.broadcast_to(band_lo.astype(f32)[None, :], (RB_DEV, 32)),
+            jnp.broadcast_to(band_hi.astype(f32)[None, :], (RB_DEV, 32)),
+        ],
+        axis=1,
     )
-    gain = jnp.stack([scale * jnp.cos(phase), scale * jnp.sin(phase)])
-    return jnp.broadcast_to(gain.reshape(2, 3, RB_DEV, 1), (2, 3, RB_DEV, LANES))
 
 
 def per_device(echoes, range_phase, azimuth_rate, band_lo, band_hi, band_map, recon_filter):
@@ -482,21 +561,37 @@
         jnp.where(band_map[None, :] == order[:, None], order[None, :], 0), axis=1
     )
     scalars = jnp.concatenate([band_map, jnp.stack([own_index, block_index]), row_of_band])
-    windows = compress(echoes, jnp.asarray(range_tables()))
+    groups = [
+        [(PAIR * i + h) * CHANS + d for h in range(PAIR) for d in range(CHANS)]
+        for i in range(N_PULSE // PAIR)
+    ]
+
+    def exchange(values):
+        return lax.all_to_all(
+            values,
+            ("pulse", "chan"),
+            split_axis=0,
+            concat_axis=0,
+            axis_index_groups=groups,
+            tiled=True,
+        )
+
+    windows, zeros = compress(echoes, jnp.asarray(range_tables()))
     turned = lax.all_to_all(windows, "pulse", split_axis=0, concat_axis=0, tiled=True)
-    gain = window_gain(range_phase, band_lo, band_hi, block_index)
-    rates = jnp.broadcast_to(azimuth_rate[:, None], (RB_DEV, LANES))
-    filt, cos_p, sin_p, base, last_lanes, last_twiddle, first_twiddle = prepare(
+    first_bin = (block_index - 1 + jnp.bitwise_and(block_index, 1)) * RB_DEV
+    given = zeros + block_values(azimuth_rate, band_lo, band_hi)
+    other = lax.ppermute(given, "pulse", [(b, b ^ 1) for b in range(N_PULSE)])
+    filt, last_lanes, last_twiddle, base, first_twiddle = tables(
         scalars,
-        rates,
-        gain,
+        window_gain(range_phase, first_bin),
         jnp.asarray(twiddle_tables()),
         recon_filter.reshape(2 * CHANS * CHANS, PULSES),
     )
-    doppler = spectra(turned, jnp.asarray(lane_tables()), first_twiddle)
-    gathered = lax.all_to_all(doppler, "chan", split_axis=0, concat_axis=0, tiled=True)
-    summed = merge(scalars, gathered, filt, cos_p, sin_p, base)
-    combined = lax.all_to_all(summed, "chan", split_axis=0, concat_axis=0, tiled=True)
+    cos_p, sin_p, mask = phases(scalars, given, other)
+    doppler = spectra(turned, jnp.asarray(lane_tables()), first_twiddle, mask)
+    gathered = exchange(doppler)
+    summed = merge(scalars, gathered, filt, cos_p, sin_p, base, mask)
+    combined = exchange(summed)
     return image(combined, last_lanes, last_twiddle)
 
 

time: 63.7 us -> 61.6 us (0.967)
  waiting for transfers between devices: 8.89 us -> 2.66 us
  starting transfers between devices: 17.1 us -> 20.2 us
  other arithmetic: 0.33 us -> 1.01 us
    all_to_all x1, waiting for transfers between devices: 8.89 us -> 2.66 us  [per_device(): lax.all_to_all(windows, 'pulse', split_axis=0, concat_axis=0, tiled=True)]
    ppermute x0 -> x1, starting transfers between devices: none -> 2.91 us  [per_device(): other = lax.ppermute(given, 'pulse', [(b, b ^ 1) for b in range(N_PULSE)])]
    unnamed x16 -> x10, local copies, waits for them, and re-layouts: 1.64 us -> 0.03 us
    reshape x1, local copies, waits for them, and re-layouts: 0.42 us -> 1.46 us  [per_device(): recon_filter.reshape(2 * CHANS * CHANS, PULSES)]
    add x0 -> x1, other arithmetic: none -> 0.68 us  [per_device(): given = zeros + block_values(azimuth_rate, band_lo, band_hi)]
    pallas_call x3 -> x4, Pallas kernels: 6.67 us -> 7.03 us  [the longest x1 3.71 us: compress(): pl.pallas_call(compress_kernel, in_specs=[pl.BlockSpec(memory_space=pl.AN...]
  transfers between devices with their start and end apart: 1 -> 2, of which waited for: 1 -> 1; matrix products, arithmetic and copies ran while one was open for 2% -> 5% of each run, Pallas kernels for 3% -> 4%
where the time goes in v2:
time: 61.6 us; the launch traced here: 61.2 us
  blocking collectives  24.5 us (40%)
  starting transfers between devices  20.2 us (33%)
  Pallas kernels  9.43 us (15%)
  waiting for transfers between devices  2.66 us (4%)
  local copies, waits for them, and re-layouts  1.95 us (3%)
  between operations  1.47 us (2%)
  other arithmetic  1.01 us (2%)
    all_to_all x2, blocking collectives, exchange(): lax.all_to_all(values, ('pulse', 'chan'), split_axis=0, concat_axis=0, ax...  24.5 us
    all_to_all x1, starting transfers between devices, per_device(): lax.all_to_all(windows, 'pulse', split_axis=0, concat_axis=0, tiled=True)  17.3 us
    pallas_call x1, Pallas kernels, compress(): pl.pallas_call(compress_kernel, in_specs=[pl.BlockSpec(memory_space=pl.AN...  3.71 us
    ppermute x1, starting transfers between devices, per_device(): other = lax.ppermute(given, 'pulse', [(b, b ^ 1) for b in range(N_PULSE)])  2.91 us
    all_to_all x1, waiting for transfers between devices, per_device(): lax.all_to_all(windows, 'pulse', split_axis=0, concat_axis=0, tiled=True)  2.66 us
    pallas_call x1, Pallas kernels, tables(): pl.pallas_call(tables_kernel, in_specs=[pl.BlockSpec(memory_space=pltpu.S...  1.61 us
    reshape x1, local copies, waits for them, and re-layouts, per_device(): recon_filter.reshape(2 * CHANS * CHANS, PULSES)  1.46 us
    pallas_call x1, Pallas kernels, merge(): pl.pallas_call(merge_kernel, in_specs=[pl.BlockSpec(memory_space=pltpu.SM...  1.4 us
  transfers between devices with their start and end apart: 2, of which 1 were waited for; matrix products, arithmetic and copies ran while one was open for 5% of the time, Pallas kernels for 4%

profile of v2, /device:TPU:1, one launch (start us, length us, event | category | flops | bytes accessed | tf_op | source)
XLA Modules:
  0.0 61.2 jit_solution(5323702249328844286)
XLA Ops:
  0.0 0.0 copy-start.3
  0.0 3.7 %compress.1 = (bf16[32,2,8,256]{3,2,1,0:T(8,128)(2,1)}, f32[8,128]{1,0:T(8,128)}) custom-call(bf16[2,1,64,4096]{3,2,1,0:T(8,128)(2,1)} %echo_hbm.1, bf16[4,256,1024]{2,1,0:T(8,128)(2,1)} %constant.30.clone.table_hbm), custom_call_target="tpu_custom_call" | custom-call | flops 536870912 | bytes 4194304 | tf_op jit(solution)/shard_map/compress/pallas_call | solution.py:159
  3.7 0.0 copy-start.4
  3.7 0.0 copy-start
  3.7 17.3 %all-to-all-start = ((bf16[64,8,256]{2,1,0:T(8,128)(2,1)}), bf16[64,8,256]{2,1,0:T(8,128)(2,1)S(1)}, u32[]{:S(2)}, u32[]{:S(2)}) async-start(bf16[64,8,256]{2,1,0:T(8,128)(2,1)} %bitcast.7), calls=%async_computation | async-start | bytes 524288 | tf_op jit(solution)/shard_map/all_to_all | solution.py:580
  21.0 0.0 copy-start.1
  22.4 0.1 pad.6.clone
  22.5 0.1 pad.7.clone
  22.6 0.0 copy-done.3
  22.6 0.1 broadcast_in_dim.48
  22.6 0.7 %maximum_add_fusion.own_ref = f32[8,128]{1,0:T(8,128)S(1)} fusion(f32[8,128]{1,0:T(8,128)} %get-tuple-element.17, f32[8,64]{1,0:T(8,128)S(1)} %broadcast_in_dim.48, f32[128]{0:T(128)S(1)} %pad.7.clone, f32[128]{0:T(128)S(1)} %pad.6.clone), kind=kLoop, calls=%fused_computation | loop fusion | flops 3072 | bytes 11264 | tf_op jit(solution)/shard_map/add | solution.py:582
  23.3 2.9 %collective-permute-start = (f32[8,128]{1,0:T(8,128)S(1)}, f32[8,128]{1,0:T(8,128)S(1)}, u32[]{:S(2)}, u32[]{:S(2)}) collective-permute-start(f32[8,128]{1,0:T(8,128)S(1)} %maximum_add_fusion.own_ref), channel_id=1, source_target_pairs={{0,8},{8,0},{16,24},{24,16},{32,40},{40,32},{48,56},{56,48},{64,72... | collective-permute-start | bytes 12296 | tf_op jit(solution)/shard_map/ppermute | solution.py:583
  26.2 0.0 copy-done.2
  26.2 0.1 cosine_multiply_fusion
  26.4 0.1 stack.17
  26.5 0.1 stack.18
  26.5 1.5 %reshape.16.filter_ref = bf16[128,4096]{1,0:T(8,128)(2,1)S(1)} reshape(bf16[8,8,2,4096]{3,2,1,0:T(2,128)(2,1)} %param.16) | data formatting | bytes 2097152 | tf_op jit(solution)/shard_map/reshape | solution.py:588
  28.0 0.0 copy-done.4
  28.0 0.1 select_reduce_fusion
  28.1 0.1 pad_add_fusion.scalars
  28.2 0.1 broadcast_in_dim.47.gain_ref
  28.3 0.0 copy-done
  28.3 1.6 %tables.1 = (f32[2,128,128]{2,1,0:T(8,128)S(1)}, bf16[256,512]{1,0:T(8,128)(2,1)S(1)}, f32[256,256]{1,0:T(8,128)S(1)}, f32[8,32,128]{2,1,0:T(8,128)S(1)}, f32[2,256,256]{2,1,0:T(8,128)S(1)}) custom-call(s32[18]{0:T(128)S(1)} %pad_add_fusion.scalars, f32[2,2,8,128]{3,2,1,0:T(8,128)S(1)} %broadcast_in_dim.47.gain_ref, f32[256,256]{1,0:T(8,128)S(1)} %copy-done, ...), custom_call_target="tpu_custom_call" | custom-call | flops 268435456 | bytes 2097152 | tf_op jit(solution)/shard_map/tables/pallas_call | solution.py:352
  29.9 0.0 collective-permute-done.other_ref
  29.9 1.1 %phases.1 = (f32[8,32,128]{2,1,0:T(8,128)S(1)}, f32[8,32,128]{2,1,0:T(8,128)S(1)}, f32[2,3,8,128]{3,2,1,0:T(8,128)S(1)}) custom-call(s32[18]{0:T(128)S(1)} %pad_add_fusion.scalars, f32[8,128]{1,0:T(8,128)S(1)} %maximum_add_fusion.own_ref, f32[8,128]{1,0:T(8,128)S(1)} %collective-permute-done.other_ref), custom_call_target="tpu_custom_call" | custom-call | flops 16777216 | bytes 1048576 | tf_op jit(solution)/shard_map/phases/pallas_call | solution.py:397
  31.0 2.7 %all-to-all-done.turned_ref = bf16[64,8,256]{2,1,0:T(8,128)(2,1)S(1)} async-done(((bf16[64,8,256]{2,1,0:T(8,128)(2,1)}), bf16[64,8,256]{2,1,0:T(8,128)(2,1)S(1)}, u32[]{:S(2)}, u32[]{:S(2)}) %all-to-all-start) | async-done | bytes 262176 | tf_op jit(solution)/shard_map/all_to_all | solution.py:580
  33.7 0.0 copy-done.1
  33.7 0.6 spectra.1
  34.3 14.9 %all_to_all.15.gathered_ref = bf16[16,32,256]{2,1,0:T(8,128)(2,1)S(1)} all-to-all(bf16[16,32,256]{2,1,0:T(8,128)(2,1)S(1)} %spectra.1), channel_id=1, replica_groups={{0,1,2,3,4,5,6,7,8,9,10,11,12,13,14,15},{16,17,18,19,20,21,22,23,24,25,..., dimensions={0} | all-to-all | bytes 524288 | tf_op jit(solution)/shard_map/all_to_all | solution.py:570
  49.2 1.4 %merge.1 = bf16[16,16,256]{2,1,0:T(8,128)(2,1)S(1)} custom-call(s32[18]{0:T(128)S(1)} %pad_add_fusion.scalars, bf16[16,32,256]{2,1,0:T(8,128)(2,1)S(1)} %all_to_all.15.gathered_ref, f32[2,128,128]{2,1,0:T(8,128)S(1)} %get-tuple-element.19.filt_ref, f32[8,32,128]{2,1,0:T(8,128)S(1)} %get-tuple-element.20.cos_ref, ...), custom_call_target="tpu_custom_call" | custom-call | flops 16777216 | bytes 2097152 | tf_op jit(solution)/shard_map/merge/pallas_call | solution.py:488
  50.6 9.6 %all_to_all.16.combined_ref = bf16[16,16,256]{2,1,0:T(8,128)(2,1)S(1)} all-to-all(bf16[16,16,256]{2,1,0:T(8,128)(2,1)S(1)} %merge.1), channel_id=1, replica_groups={{0,1,2,3,4,5,6,7,8,9,10,11,12,13,14,15},{16,17,18,19,20,21,22,23,24,25,..., dimensions={0} | all-to-all | bytes 262144 | tf_op jit(solution)/shard_map/all_to_all | solution.py:570
  60.2 1.0 %image.1 = f32[2,8,4096]{2,1,0:T(8,128)} custom-call(bf16[16,16,256]{2,1,0:T(8,128)(2,1)S(1)} %all_to_all.16.combined_ref, bf16[256,512]{1,0:T(8,128)(2,1)S(1)} %get-tuple-element.23.lanes_ref, f32[256,256]{1,0:T(8,128)S(1)} %get-tuple-element.24.twiddle_ref), custom_call_target="tpu_custom_call" | custom-call | flops 67108864 | bytes 2097152 | tf_op jit(solution)/shard_map/image/pallas_call | solution.py:522
  (4 shorter events, 0.0 us)
Async XLA Ops:
  0.0 22.6 %copy-start.3 = (f32[8]{0:T(128)S(1)}, f32[8]{0:T(128)}, u32[]{:S(2)}) copy-start(f32[8]{0:T(128)} %param.12) | copy-start | bytes 100
  0.0 26.2 %copy-start.2 = (f32[512]{0:T(512)S(1)}, f32[512]{0:T(512)}, u32[]{:S(2)}) copy-start(f32[512]{0:T(512)} %param.11) | copy-start | bytes 6148
  3.7 24.3 %copy-start.4 = (s32[8]{0:T(128)S(1)}, s32[8]{0:T(128)}, u32[]{:S(2)}) copy-start(s32[8]{0:T(128)} %param.15) | copy-start | bytes 100
  3.7 24.6 %copy-start = (f32[256,256]{1,0:T(8,128)S(1)}, f32[256,256]{1,0:T(8,128)}, u32[]{:S(2)}) copy-start(f32[256,256]{1,0:T(8,128)} %constant.31.clone.turns_ref) | copy-start | bytes 786436
  3.7 29.9 %all-to-all-start = ((bf16[64,8,256]{2,1,0:T(8,128)(2,1)}), bf16[64,8,256]{2,1,0:T(8,128)(2,1)S(1)}, u32[]{:S(2)}, u32[]{:S(2)}) async-start(bf16[64,8,256]{2,1,0:T(8,128)(2,1)} %bitcast.7), calls=%async_computation | async-start | bytes 524288 | tf_op jit(solution)/shard_map/all_to_all | solution.py:580
  21.0 12.7 %copy-start.1 = (bf16[256,512]{1,0:T(8,128)(2,1)S(1)}, bf16[256,512]{1,0:T(8,128)(2,1)}, u32[]{:S(2)}) copy-start(bf16[256,512]{1,0:T(8,128)(2,1)} %constant.32.clone.lanes_ref) | copy-start | bytes 786436
  23.3 6.6 %collective-permute-start = (f32[8,128]{1,0:T(8,128)S(1)}, f32[8,128]{1,0:T(8,128)S(1)}, u32[]{:S(2)}, u32[]{:S(2)}) collective-permute-start(f32[8,128]{1,0:T(8,128)S(1)} %maximum_add_fusion.own_ref), channel_id=1, source_target_pairs={{0,8},{8,0},{16,24},{24,16},{32,40},{40,32},{48,56},{56,48},{64,72... | collective-permute-start | bytes 12296 | tf_op jit(solution)/shard_map/ppermute | solution.py:583

commit v3 on v2

--- a/solution.py
+++ b/solution.py
@@ -22,9 +22,11 @@
 LANES = 128
 ROWS = PULSES // LANES
 PAIR = 2
+LAST = PAIR * CHANS - 1
 OWN = ROWS // (PAIR * CHANS)
 OUT_ROWS = PAIR * RB_DEV * OWN
 PULSES_DEV = PULSES // N_PULSE
+STRIP = 32
 curvature = 300.0
 
 f32 = jnp.float32
@@ -37,14 +39,22 @@
     return high, low
 
 
-def range_tables():
-    tables = []
-    sample = np.arange(FOLD)
-    for rho in range(RADIX):
-        bins = np.array([8 * block + 4 * h + rho for h in range(2) for block in range(N_PULSE)])
-        angle = (bins[:, None] * sample[None, :]) % NS * (2.0 * math.pi / NS)
-        tables.append(np.concatenate([np.cos(angle), np.sin(angle)], axis=0))
-    return np.stack(tables).astype(np.float32).astype(bf16)
+def range_table(bins, samples):
+    angle = (np.asarray(bins)[:, None] * np.arange(samples)[None, :]) % NS * (2.0 * math.pi / NS)
+    table = np.concatenate([np.cos(angle), np.sin(angle)], axis=0)
+    return table.astype(np.float32).astype(bf16)
+
+
+def odd_tables():
+    blocks = RB_DEV * np.arange(N_PULSE)[::-1]
+    return np.stack(
+        [range_table(np.concatenate([blocks + r, blocks + 4 + r]), FOLD) for r in (1, 3)]
+    )
+
+
+def even_tables():
+    blocks = RB_DEV * np.arange(N_PULSE)[::-1]
+    return np.stack([range_table(blocks + 2 * e, FOLD // 2) for e in range(4)])
 
 
 def lane_tables():
@@ -76,107 +86,135 @@
 
 def compress_kernel(
     echo_hbm,
-    table_hbm,
+    odd_hbm,
+    even_hbm,
     out_ref,
     zero_ref,
     echo,
-    table,
-    folded,
+    odd,
+    even,
+    odd_sums,
+    even_sums,
     bins,
     echo_sem,
     table_sem,
 ):
-    def echo_copy(part):
-        return pltpu.make_async_copy(echo_hbm.at[part, 0], echo.at[part], echo_sem.at[part])
-
-    def table_copy(residue):
+    def echo_copy(part, strip):
+        rows = pl.ds(strip * STRIP, STRIP)
         return pltpu.make_async_copy(
-            table_hbm.at[residue], table.at[residue], table_sem.at[residue]
+            echo_hbm.at[part, 0, rows], echo.at[part, rows], echo_sem.at[part, strip]
         )
 
-    for part in range(2):
-        echo_copy(part).start()
-    for residue in range(RADIX):
-        table_copy(residue).start()
-    for part in range(2):
-        echo_copy(part).wait()
-
-    def put(residue, part, rows, cols, values):
+    table_copies = [
+        pltpu.make_async_copy(odd_hbm, odd, table_sem.at[0]),
+        pltpu.make_async_copy(even_hbm, even, table_sem.at[1]),
+    ]
+    for strip in range(PULSES_DEV // STRIP):
+        for part in range(2):
+            echo_copy(part, strip).start()
+    for copy in table_copies:
+        copy.start()
+
+    def put(folded, at, part, rows, left, values):
         high, low = split(values)
-        folded[residue, part * 64 + rows : part * 64 + rows + 16, cols] = high
-        folded[residue, 128 + part * 64 + rows : 128 + part * 64 + rows + 16, cols] = low
+        cols = slice(left, left + values.shape[1])
+        folded[at, part * 64 + rows : part * 64 + rows + 16, cols] = high
+        folded[at, 128 + part * 64 + rows : 128 + part * 64 + rows + 16, cols] = low
 
     width = 256
+    half = FOLD // 2
     for rows in range(0, PULSES_DEV, 16):
-        for left in range(0, FOLD, width):
-            cols = slice(left, left + width)
-            pieces = [
-                [
-                    echo[part, rows : rows + 16, a * FOLD + left : a * FOLD + left + width].astype(f32)
-                    for a in range(RADIX)
+        if rows % STRIP == 0:
+            for part in range(2):
+                echo_copy(part, rows // STRIP).wait()
+        for left in range(0, half, width):
+            z = [[None] * 4 for _ in range(2)]
+            for upper in range(2):
+                at = left + upper * half
+                pieces = [
+                    [
+                        echo[part, rows : rows + 16, a * FOLD + at : a * FOLD + at + width].astype(f32)
+                        for a in range(RADIX)
+                    ]
+                    for part in range(2)
                 ]
-                for part in range(2)
-            ]
-            (re0, re1, re2, re3), (im0, im1, im2, im3) = pieces
+                (re0, re1, re2, re3), (im0, im1, im2, im3) = pieces
+                re_s, re_t, im_s, im_t = re0 - re2, re1 - re3, im0 - im2, im1 - im3
+                put(odd_sums, 0, 0, rows, at, re_s + im_t)
+                put(odd_sums, 0, 1, rows, at, im_s - re_t)
+                put(odd_sums, 1, 0, rows, at, re_s - im_t)
+                put(odd_sums, 1, 1, rows, at, im_s + re_t)
+                z[0][upper], z[0][2 + upper] = re0 + re2, re1 + re3
+                z[1][upper], z[1][2 + upper] = im0 + im2, im1 + im3
+            (re0, re1, re2, re3), (im0, im1, im2, im3) = z
             re_s, re_t, im_s, im_t = re0 + re2, re1 + re3, im0 + im2, im1 + im3
-            put(0, 0, rows, cols, re_s + re_t)
-            put(0, 1, rows, cols, im_s + im_t)
-            put(2, 0, rows, cols, re_s - re_t)
-            put(2, 1, rows, cols, im_s - im_t)
+            put(even_sums, 0, 0, rows, left, re_s + re_t)
+            put(even_sums, 0, 1, rows, left, im_s + im_t)
+            put(even_sums, 2, 0, rows, left, re_s - re_t)
+            put(even_sums, 2, 1, rows, left, im_s - im_t)
             re_s, re_t, im_s, im_t = re0 - re2, re1 - re3, im0 - im2, im1 - im3
-            put(1, 0, rows, cols, re_s + im_t)
-            put(1, 1, rows, cols, im_s - re_t)
-            put(3, 0, rows, cols, re_s - im_t)
-            put(3, 1, rows, cols, im_s + re_t)
-
-    for residue in range(RADIX):
-        table_copy(residue).wait()
+            put(even_sums, 1, 0, rows, left, re_s + im_t)
+            put(even_sums, 1, 1, rows, left, im_s - re_t)
+            put(even_sums, 3, 0, rows, left, re_s - im_t)
+            put(even_sums, 3, 1, rows, left, im_s + re_t)
+
+    for copy in table_copies:
+        copy.wait()
     zero_ref[...] = jnp.zeros((RB_DEV, LANES), f32)
-    sign = jnp.where(lane_index((128, LANES)) < 64, 1.0, -1.0)
-    for residue in range(RADIX):
+
+    def transform(table, folded):
         sums = lax.dot_general(
-            table[residue], folded[residue], (((1,), (1,)), ((), ())), preferred_element_type=f32
+            table, folded, (((1,), (1,)), ((), ())), preferred_element_type=f32
         )
         sums = sums[:, :LANES] + sums[:, LANES:]
-        comp = sums[:128] + sign * pltpu.roll(sums[128:], 64, 1)
+        count = sums.shape[0] // 2
+        sign = jnp.where(lane_index((count, LANES)) < 64, 1.0, -1.0)
+        return sums[:count] + sign * pltpu.roll(sums[count:], 64, 1)
+
+    for at in range(2):
+        comp = transform(odd[at], odd_sums[at])
         for h in range(2):
-            bins[pl.ds(4 * h + residue, N_PULSE, stride=RB_DEV), :] = comp[
+            bins[pl.ds(4 * h + 2 * at + 1, N_PULSE, stride=RB_DEV), :] = comp[
                 h * N_PULSE : (h + 1) * N_PULSE
             ]
+    for e in range(4):
+        bins[pl.ds(2 * e, N_PULSE, stride=RB_DEV), :] = transform(even[e], even_sums[e])
     own = bins[...].astype(bf16).reshape(N_PULSE // 2, 2, RB_DEV, LANES)
-    even, odd = own[:, 0], own[:, 1]
+    odds, evens = own[:, 0], own[:, 1]
     edge = jnp.zeros((1, RB_DEV, LANES), bf16)
     last = N_PULSE // 2 - 1
-    out_ref[0:1, 0, :, :LANES] = edge
-    out_ref[1:, 0, :, :LANES] = odd[:last]
-    out_ref[:, 0, :, LANES:] = even
-    out_ref[:, 1, :, :LANES] = odd
-    out_ref[:last, 1, :, LANES:] = even[1:]
-    out_ref[last:, 1, :, LANES:] = edge
-
-
-def compress(echoes, tables):
+    out_ref[:, 0, :, :LANES] = odds
+    out_ref[0:1, 0, :, LANES:] = edge
+    out_ref[1:, 0, :, LANES:] = evens[:last]
+    out_ref[:last, 1, :, :LANES] = odds[1:]
+    out_ref[last:, 1, :, :LANES] = edge
+    out_ref[:, 1, :, LANES:] = evens
+
+
+def compress(echoes, odd, even):
     windows, zeros = pl.pallas_call(
         compress_kernel,
-        in_specs=[pl.BlockSpec(memory_space=pl.ANY)] * 2,
+        in_specs=[pl.BlockSpec(memory_space=pl.ANY)] * 3,
         out_shape=(
             jax.ShapeDtypeStruct((N_PULSE // 2, 2, RB_DEV, 2 * LANES), bf16),
             jax.ShapeDtypeStruct((RB_DEV, LANES), f32),
         ),
         scratch_shapes=[
             pltpu.VMEM((2, PULSES_DEV, NS), bf16),
-            pltpu.VMEM((RADIX, 256, FOLD), bf16),
-            pltpu.VMEM((RADIX, 256, FOLD), bf16),
+            pltpu.VMEM((2, 256, FOLD), bf16),
+            pltpu.VMEM((4, 128, FOLD // 2), bf16),
+            pltpu.VMEM((2, 256, FOLD), bf16),
+            pltpu.VMEM((4, 256, FOLD // 2), bf16),
             pltpu.VMEM((NR, LANES), f32),
+            pltpu.SemaphoreType.DMA((2, PULSES_DEV // STRIP)),
             pltpu.SemaphoreType.DMA((2,)),
-            pltpu.SemaphoreType.DMA((RADIX,)),
         ],
         compiler_params=pltpu.CompilerParams(vmem_limit_bytes=60 << 20),
         cost_estimate=pl.CostEstimate(
-            flops=2 * RADIX * 256 * 256 * FOLD, bytes_accessed=4 << 20, transcendentals=0
+            flops=6 * 256 * 256 * FOLD, bytes_accessed=4 << 20, transcendentals=0
         ),
         name="compress",
-    )(echoes, tables)
+    )(echoes, odd, even)
     return windows.reshape(N_PULSE, RB_DEV, 2 * LANES), zeros
 
 
@@ -236,8 +274,8 @@
         cols = slice(group * LANES, (group + 1) * LANES)
 
         def load(p_hi):
-            even = turned_ref[2 * p_hi, :, cols].astype(f32)
-            odd = turned_ref[2 * p_hi + 1, :, cols].astype(f32)
+            even = turned_ref[N_PULSE - 1 - 2 * p_hi, :, cols].astype(f32)
+            odd = turned_ref[N_PULSE - 2 - 2 * p_hi, :, cols].astype(f32)
             real_x = jnp.where(low_half, even, pltpu.roll(odd, 64, 1))
             imag_x = jnp.where(low_half, pltpu.roll(even, 64, 1), odd)
             return (imag_x, real_x)
@@ -282,7 +320,7 @@
     shape = (OUT_ROWS, LANES)
     row = lax.broadcasted_iota(jnp.int32, shape, 0)
     lane = lax.broadcasted_iota(jnp.int32, shape, 1)
-    digit = OWN * (member * CHANS + scalars[CHANS]) + lax.shift_right_logical(row, 4)
+    digit = OWN * (LAST - member * CHANS - scalars[CHANS]) + lax.shift_right_logical(row, 4)
     bins = (block - member) * RB_DEV + jnp.bitwise_and(row, 15)
     return 32 * lane + digit, bins.astype(f32), jnp.bitwise_and(row, 7).astype(f32)
 
@@ -303,7 +341,7 @@
     first_ref,
 ):
     chan = scalars[CHANS]
-    first_digit = OWN * (jnp.bitwise_and(scalars[CHANS + 1], 1) * CHANS + chan)
+    first_digit = OWN * (LAST - jnp.bitwise_and(scalars[CHANS + 1], 1) * CHANS - chan)
     tw_cos = turns_ref[:, :LANES].reshape(ROWS, RB_DEV, LANES)
     tw_sin = turns_ref[:, LANES:].reshape(ROWS, RB_DEV, LANES)
     for group in range(2):
@@ -445,7 +483,7 @@
                 f_re = jnp.broadcast_to(filters[2 * c : 2 * c + 1], (RB_DEV, LANES))
                 f_im = jnp.broadcast_to(filters[2 * c + 1 : 2 * c + 2], (RB_DEV, LANES))
                 for part in needed:
-                    source = (part // 2) * CHANS + c
+                    source = LAST - (part // 2) * CHANS - c
                     at = (part % 2) * 16 + digit * RB_DEV
                     s_re = wide[source, at : at + RB_DEV, :LANES]
                     s_im = wide[source, at : at + RB_DEV, LANES:]
@@ -479,8 +517,8 @@
     for h in range(PAIR):
         results = fft8([(bands[k, 0, h], bands[k, 1, h]) for k in range(CHANS)])
         for a in range(CHANS):
-            out_ref[h * CHANS + a, :, :LANES] = results[a][0].astype(bf16)
-            out_ref[h * CHANS + a, :, LANES:] = results[a][1].astype(bf16)
+            out_ref[LAST - h * CHANS - a, :, :LANES] = results[a][0].astype(bf16)
+            out_ref[LAST - h * CHANS - a, :, LANES:] = results[a][1].astype(bf16)
 
 
 def merge(scalars, gathered, filt, cos_p, sin_p, base, mask):
@@ -562,7 +600,7 @@
     )
     scalars = jnp.concatenate([band_map, jnp.stack([own_index, block_index]), row_of_band])
     groups = [
-        [(PAIR * i + h) * CHANS + d for h in range(PAIR) for d in range(CHANS)]
+        [(PAIR * i + h) * CHANS + d for h in range(PAIR) for d in range(CHANS)][::-1]
         for i in range(N_PULSE // PAIR)
     ]
 
@@ -576,8 +614,15 @@
             tiled=True,
         )
 
-    windows, zeros = compress(echoes, jnp.asarray(range_tables()))
-    turned = lax.all_to_all(windows, "pulse", split_axis=0, concat_axis=0, tiled=True)
+    windows, zeros = compress(echoes, jnp.asarray(odd_tables()), jnp.asarray(even_tables()))
+    turned = lax.all_to_all(
+        windows,
+        "pulse",
+        split_axis=0,
+        concat_axis=0,
+        axis_index_groups=[list(range(N_PULSE))[::-1]],
+        tiled=True,
+    )
     first_bin = (block_index - 1 + jnp.bitwise_and(block_index, 1)) * RB_DEV
     given = zeros + block_values(azimuth_rate, band_lo, band_hi)
     other = lax.ppermute(given, "pulse", [(b, b ^ 1) for b in range(N_PULSE)])

time: 61.6 us -> 55.2 us (0.90)
  blocking collectives: 24.5 us -> 21.2 us
  waiting for transfers between devices: 2.66 us -> 0.01 us
  other arithmetic: 1.01 us -> 0.33 us
    all_to_all x2, blocking collectives: 24.5 us -> 21.2 us  [exchange(): lax.all_to_all(values, ('pulse', 'chan'), split_axis=0, concat_axis=0, ax...]
    all_to_all x1, waiting for transfers between devices: 2.66 us -> 0.01 us  [per_device(): lax.all_to_all(windows, 'pulse', split_axis=0, concat_axis=0, axis_index_...]
    unnamed x10 -> x14, local copies, waits for them, and re-layouts: 0.03 us -> 1.48 us
    reshape x1, local copies, waits for them, and re-layouts: 1.46 us -> 0.42 us  [per_device(): recon_filter.reshape(2 * CHANS * CHANS, PULSES)]
    add x1, other arithmetic: 0.68 us -> 0.01 us  [per_device(): given = zeros + block_values(azimuth_rate, band_lo, band_hi)]
  transfers between devices with their start and end apart: 2 -> 2, of which waited for: 1 -> 0; matrix products, arithmetic and copies ran while one was open for 5% -> 2% of each run, Pallas kernels for 4% -> 5%
where the time goes in v3:
time: 55.2 us; the launch traced here: 54.9 us
  blocking collectives  21.2 us (38%)
  starting transfers between devices  20.4 us (37%)
  Pallas kernels  9.17 us (17%)
  local copies, waits for them, and re-layouts  2.36 us (4%)
  between operations  1.43 us (3%)
    all_to_all x2, blocking collectives, exchange(): lax.all_to_all(values, ('pulse', 'chan'), split_axis=0, concat_axis=0, ax...  21.2 us
    all_to_all x1, starting transfers between devices, per_device(): lax.all_to_all(windows, 'pulse', split_axis=0, concat_axis=0, axis_index_...  17.3 us
    pallas_call x1, Pallas kernels, compress(): pl.pallas_call(compress_kernel, in_specs=[pl.BlockSpec(memory_space=pl.AN...  3.45 us
    ppermute x1, starting transfers between devices, per_device(): other = lax.ppermute(given, 'pulse', [(b, b ^ 1) for b in range(N_PULSE)])  3.07 us
    pallas_call x1, Pallas kernels, tables(): pl.pallas_call(tables_kernel, in_specs=[pl.BlockSpec(memory_space=pltpu.S...  1.6 us
    unnamed x14, local copies, waits for them, and re-layouts  1.48 us
    pallas_call x1, Pallas kernels, merge(): pl.pallas_call(merge_kernel, in_specs=[pl.BlockSpec(memory_space=pltpu.SM...  1.41 us
    pallas_call x1, Pallas kernels, phases(): pl.pallas_call(phases_kernel, in_specs=[pl.BlockSpec(memory_space=pltpu.S...  1.11 us
  transfers between devices with their start and end apart: 2, of which 0 were waited for; matrix products, arithmetic and copies ran while one was open for 2% of the time, Pallas kernels for 5%

profile of v3, /device:TPU:1, one launch (start us, length us, event | category | flops | bytes accessed | tf_op | source)
XLA Modules:
  0.0 54.9 jit_solution(14918909345779223394)
XLA Ops:
  0.0 3.5 %compress.1 = (bf16[32,2,8,256]{3,2,1,0:T(8,128)(2,1)}, f32[8,128]{1,0:T(8,128)}) custom-call(bf16[2,1,64,4096]{3,2,1,0:T(8,128)(2,1)} %echo_hbm.1, bf16[2,256,1024]{2,1,0:T(8,128)(2,1)} %constant.32.clone.odd_hbm, bf16[4,128,512]{2,1,0:T(8,128)(2,1)} %constant.33.clone.even_hbm), custom_call_target="tpu_custom_call" | custom-call | flops 402653184 | bytes 4194304 | tf_op jit(solution)/shard_map/compress/pallas_call | solution.py:195
  3.5 0.0 copy-start.5
  3.5 17.3 %all-to-all-start = ((bf16[64,8,256]{2,1,0:T(8,128)(2,1)}), bf16[64,8,256]{2,1,0:T(8,128)(2,1)S(1)}, u32[]{:S(2)}, u32[]{:S(2)}) async-start(bf16[64,8,256]{2,1,0:T(8,128)(2,1)} %bitcast.7), calls=%async_computation | async-start | bytes 524288 | tf_op jit(solution)/shard_map/all_to_all | solution.py:618
  22.1 0.1 pad.6.clone
  22.2 0.1 pad.7.clone
  22.2 0.0 copy-done.5
  22.2 0.1 broadcast_in_dim.48
  22.3 0.5 copy-done.3
  22.8 3.1 %collective-permute-start = (f32[8,128]{1,0:T(8,128)S(1)}, f32[8,128]{1,0:T(8,128)S(1)}, u32[]{:S(2)}, u32[]{:S(2)}) collective-permute-start(f32[8,128]{1,0:T(8,128)S(1)} %maximum_add_fusion.own_ref), channel_id=1, source_target_pairs={{0,8},{8,0},{16,24},{24,16},{32,40},{40,32},{48,56},{56,48},{64,72... | collective-permute-start | bytes 12296 | tf_op jit(solution)/shard_map/ppermute | solution.py:628
  25.9 0.0 copy-start.4
  25.9 0.7 %copy-done.4 = f32[512]{0:T(512)S(1)} copy-done((f32[512]{0:T(512)S(1)}, f32[512]{0:T(512)}, u32[]{:S(2)}) %copy-start.4) | copy-done | bytes 2072
  26.6 0.1 cosine_multiply_fusion
  26.7 0.1 stack.17
  26.8 0.1 stack.18
  26.9 0.0 copy-done.2
  26.9 0.4 reshape.16.filter_ref
  27.3 0.2 copy-done.6
  27.6 0.1 select_reduce_fusion
  27.7 0.1 pad_add_fusion.scalars
  27.8 0.1 broadcast_in_dim.47.gain_ref
  27.8 0.0 copy-done
  27.9 1.6 %tables.1 = (f32[2,128,128]{2,1,0:T(8,128)S(1)}, bf16[256,512]{1,0:T(8,128)(2,1)S(1)}, f32[256,256]{1,0:T(8,128)S(1)}, f32[8,32,128]{2,1,0:T(8,128)S(1)}, f32[2,256,256]{2,1,0:T(8,128)S(1)}) custom-call(s32[18]{0:T(128)S(1)} %pad_add_fusion.scalars, f32[2,2,8,128]{3,2,1,0:T(8,128)S(1)} %broadcast_in_dim.47.gain_ref, f32[256,256]{1,0:T(8,128)S(1)} %copy-done, ...), custom_call_target="tpu_custom_call" | custom-call | flops 268435456 | bytes 2097152 | tf_op jit(solution)/shard_map/tables/pallas_call | solution.py:390
  29.5 0.0 copy-start.1
  29.5 0.0 collective-permute-done.other_ref
  29.5 1.1 %phases.1 = (f32[8,32,128]{2,1,0:T(8,128)S(1)}, f32[8,32,128]{2,1,0:T(8,128)S(1)}, f32[2,3,8,128]{3,2,1,0:T(8,128)S(1)}) custom-call(s32[18]{0:T(128)S(1)} %pad_add_fusion.scalars, f32[8,128]{1,0:T(8,128)S(1)} %maximum_add_fusion.own_ref, f32[8,128]{1,0:T(8,128)S(1)} %collective-permute-done.other_ref), custom_call_target="tpu_custom_call" | custom-call | flops 16777216 | bytes 1048576 | tf_op jit(solution)/shard_map/phases/pallas_call | solution.py:435
  30.6 0.0 all-to-all-done.turned_ref
  30.6 0.0 copy-done.1
  30.6 0.6 %spectra.1 = bf16[16,32,256]{2,1,0:T(8,128)(2,1)S(1)} custom-call(bf16[64,8,256]{2,1,0:T(8,128)(2,1)S(1)} %all-to-all-done.turned_ref, bf16[256,512]{1,0:T(8,128)(2,1)S(1)} %copy-done.1, f32[2,256,256]{2,1,0:T(8,128)S(1)} %get-tuple-element.16.twiddle_ref, f32[2,3,8,128]{3,2,1,0:T(8,128)S(1)} %get-tuple-element.18.after_ref.mask_ref), custom_call_target="tpu_custom_call" | custom-call | flops 201326592 | bytes 2097152 | tf_op jit(solution)/shard_map/spectra/pallas_call | solution.py:301
  31.2 12.5 %all_to_all.15.gathered_ref = bf16[16,32,256]{2,1,0:T(8,128)(2,1)S(1)} all-to-all(bf16[16,32,256]{2,1,0:T(8,128)(2,1)S(1)} %spectra.1), channel_id=1, replica_groups={{15,14,13,12,11,10,9,8,7,6,5,4,3,2,1,0},{31,30,29,28,27,26,25,24,23,22,..., dimensions={0} | all-to-all | bytes 524288 | tf_op jit(solution)/shard_map/all_to_all | solution.py:608
  43.7 1.4 %merge.1 = bf16[16,16,256]{2,1,0:T(8,128)(2,1)S(1)} custom-call(s32[18]{0:T(128)S(1)} %pad_add_fusion.scalars, bf16[16,32,256]{2,1,0:T(8,128)(2,1)S(1)} %all_to_all.15.gathered_ref, f32[2,128,128]{2,1,0:T(8,128)S(1)} %get-tuple-element.19.filt_ref, f32[8,32,128]{2,1,0:T(8,128)S(1)} %get-tuple-element.20.cos_ref, ...), custom_call_target="tpu_custom_call" | custom-call | flops 16777216 | bytes 2097152 | tf_op jit(solution)/shard_map/merge/pallas_call | solution.py:526
  45.2 8.7 %all_to_all.16.combined_ref = bf16[16,16,256]{2,1,0:T(8,128)(2,1)S(1)} all-to-all(bf16[16,16,256]{2,1,0:T(8,128)(2,1)S(1)} %merge.1), channel_id=1, replica_groups={{15,14,13,12,11,10,9,8,7,6,5,4,3,2,1,0},{31,30,29,28,27,26,25,24,23,22,..., dimensions={0} | all-to-all | bytes 262144 | tf_op jit(solution)/shard_map/all_to_all | solution.py:608
  53.9 1.0 %image.1 = f32[2,8,4096]{2,1,0:T(8,128)} custom-call(bf16[16,16,256]{2,1,0:T(8,128)(2,1)S(1)} %all_to_all.16.combined_ref, bf16[256,512]{1,0:T(8,128)(2,1)S(1)} %get-tuple-element.23.lanes_ref, f32[256,256]{1,0:T(8,128)S(1)} %get-tuple-element.24.twiddle_ref), custom_call_target="tpu_custom_call" | custom-call | flops 67108864 | bytes 2097152 | tf_op jit(solution)/shard_map/image/pallas_call | solution.py:560
  (8 shorter events, 0.0 us)
Async XLA Ops:
  0.0 26.9 %copy-start.2 = (bf16[8,8,2,4096]{3,2,1,0:T(2,128)(2,1)S(1)}, bf16[8,8,2,4096]{3,2,1,0:T(2,128)(2,1)}, u32[]{:S(2)}) copy-start(bf16[8,8,2,4096]{3,2,1,0:T(2,128)(2,1)} %param.17) | copy-start | bytes 3145732
  3.5 18.8 %copy-start.5 = (f32[8]{0:T(128)S(1)}, f32[8]{0:T(128)}, u32[]{:S(2)}) copy-start(f32[8]{0:T(128)} %param.13) | copy-start | bytes 100
  3.5 27.1 %all-to-all-start = ((bf16[64,8,256]{2,1,0:T(8,128)(2,1)}), bf16[64,8,256]{2,1,0:T(8,128)(2,1)S(1)}, u32[]{:S(2)}, u32[]{:S(2)}) async-start(bf16[64,8,256]{2,1,0:T(8,128)(2,1)} %bitcast.7), calls=%async_computation | async-start | bytes 524288 | tf_op jit(solution)/shard_map/all_to_all | solution.py:618
  22.2 0.7 %copy-start.3 = (f32[8,128]{1,0:T(8,128)S(1)}, f32[8,128]{1,0:T(8,128)}, u32[]{:S(2)}) copy-start(f32[8,128]{1,0:T(8,128)} %get-tuple-element.17) | copy-start | bytes 12292
  22.8 6.7 %collective-permute-start = (f32[8,128]{1,0:T(8,128)S(1)}, f32[8,128]{1,0:T(8,128)S(1)}, u32[]{:S(2)}, u32[]{:S(2)}) collective-permute-start(f32[8,128]{1,0:T(8,128)S(1)} %maximum_add_fusion.own_ref), channel_id=1, source_target_pairs={{0,8},{8,0},{16,24},{24,16},{32,40},{40,32},{48,56},{56,48},{64,72... | collective-permute-start | bytes 12296 | tf_op jit(solution)/shard_map/ppermute | solution.py:628
  25.9 0.7 %copy-start.4 = (f32[512]{0:T(512)S(1)}, f32[512]{0:T(512)}, u32[]{:S(2)}) copy-start(f32[512]{0:T(512)} %param.12) | copy-start | bytes 6148
  26.9 0.7 %copy-start.6 = (s32[8]{0:T(128)S(1)}, s32[8]{0:T(128)}, u32[]{:S(2)}) copy-start(s32[8]{0:T(128)} %param.16) | copy-start | bytes 100
  26.9 1.0 %copy-start = (f32[256,256]{1,0:T(8,128)S(1)}, f32[256,256]{1,0:T(8,128)}, u32[]{:S(2)}) copy-start(f32[256,256]{1,0:T(8,128)} %constant.34.clone.turns_ref) | copy-start | bytes 786436
  29.5 1.1 %copy-start.1 = (bf16[256,512]{1,0:T(8,128)(2,1)S(1)}, bf16[256,512]{1,0:T(8,128)(2,1)}, u32[]{:S(2)}) copy-start(bf16[256,512]{1,0:T(8,128)(2,1)} %constant.35.clone.lanes_ref) | copy-start | bytes 786436

commit v4 on v3

--- a/solution.py
+++ b/solution.py
@@ -27,6 +27,8 @@
 OUT_ROWS = PAIR * RB_DEV * OWN
 PULSES_DEV = PULSES // N_PULSE
 STRIP = 32
+FIRST = 62
+BLOCK_ORDER = [(FIRST - g) % N_PULSE for g in range(N_PULSE)]
 curvature = 300.0
 
 f32 = jnp.float32
@@ -46,14 +48,14 @@
 
 
 def odd_tables():
-    blocks = RB_DEV * np.arange(N_PULSE)[::-1]
+    blocks = RB_DEV * np.array(BLOCK_ORDER)
     return np.stack(
         [range_table(np.concatenate([blocks + r, blocks + 4 + r]), FOLD) for r in (1, 3)]
     )
 
 
 def even_tables():
-    blocks = RB_DEV * np.arange(N_PULSE)[::-1]
+    blocks = RB_DEV * np.array(BLOCK_ORDER)
     return np.stack([range_table(blocks + 2 * e, FOLD // 2) for e in range(4)])
 
 
@@ -180,15 +182,13 @@
     for e in range(4):
         bins[pl.ds(2 * e, N_PULSE, stride=RB_DEV), :] = transform(even[e], even_sums[e])
     own = bins[...].astype(bf16).reshape(N_PULSE // 2, 2, RB_DEV, LANES)
-    odds, evens = own[:, 0], own[:, 1]
-    edge = jnp.zeros((1, RB_DEV, LANES), bf16)
-    last = N_PULSE // 2 - 1
-    out_ref[:, 0, :, :LANES] = odds
-    out_ref[0:1, 0, :, LANES:] = edge
-    out_ref[1:, 0, :, LANES:] = evens[:last]
-    out_ref[:last, 1, :, :LANES] = odds[1:]
-    out_ref[last:, 1, :, :LANES] = edge
-    out_ref[:, 1, :, LANES:] = evens
+    evens, odds = own[:, 0], own[:, 1]
+    edge = jnp.zeros((RB_DEV, LANES), bf16)
+    for member in range(2):
+        out_ref[:, member, :, :LANES] = odds
+        out_ref[:, member, :, LANES:] = evens
+    out_ref[FIRST // 2, 0, :, :LANES] = edge
+    out_ref[FIRST // 2, 1, :, LANES:] = edge
 
 
 def compress(echoes, odd, even):
@@ -274,8 +274,8 @@
         cols = slice(group * LANES, (group + 1) * LANES)
 
         def load(p_hi):
-            even = turned_ref[N_PULSE - 1 - 2 * p_hi, :, cols].astype(f32)
-            odd = turned_ref[N_PULSE - 2 - 2 * p_hi, :, cols].astype(f32)
+            even = turned_ref[(FIRST - 2 * p_hi) % N_PULSE, :, cols].astype(f32)
+            odd = turned_ref[(FIRST - 2 * p_hi - 1) % N_PULSE, :, cols].astype(f32)
             real_x = jnp.where(low_half, even, pltpu.roll(odd, 64, 1))
             imag_x = jnp.where(low_half, pltpu.roll(even, 64, 1), odd)
             return (imag_x, real_x)
@@ -620,7 +620,7 @@
         "pulse",
         split_axis=0,
         concat_axis=0,
-        axis_index_groups=[list(range(N_PULSE))[::-1]],
+        axis_index_groups=[BLOCK_ORDER],
         tiled=True,
     )
     first_bin = (block_index - 1 + jnp.bitwise_and(block_index, 1)) * RB_DEV

time: 55.2 us -> 55 us (level)
  blocking collectives: 21.2 us -> 20.6 us
    all_to_all x2, blocking collectives: 21.2 us -> 20.6 us  [exchange(): lax.all_to_all(values, ('pulse', 'chan'), split_axis=0, concat_axis=0, ax...]
where the time goes in v4:
time: 55 us; the launch traced here: 54.7 us
  starting transfers between devices  20.8 us (38%)
  blocking collectives  20.6 us (37%)
  Pallas kernels  9.16 us (17%)
  local copies, waits for them, and re-layouts  2.36 us (4%)
  between operations  1.43 us (3%)
    all_to_all x2, blocking collectives, exchange(): lax.all_to_all(values, ('pulse', 'chan'), split_axis=0, concat_axis=0, ax...  20.6 us
    all_to_all x1, starting transfers between devices, per_device(): lax.all_to_all(windows, 'pulse', split_axis=0, concat_axis=0, axis_index_...  17.8 us
    pallas_call x1, Pallas kernels, compress(): pl.pallas_call(compress_kernel, in_specs=[pl.BlockSpec(memory_space=pl.AN...  3.45 us
    ppermute x1, starting transfers between devices, per_device(): other = lax.ppermute(given, 'pulse', [(b, b ^ 1) for b in range(N_PULSE)])  3.07 us
    pallas_call x1, Pallas kernels, tables(): pl.pallas_call(tables_kernel, in_specs=[pl.BlockSpec(memory_space=pltpu.S...  1.59 us
    unnamed x14, local copies, waits for them, and re-layouts  1.48 us
    pallas_call x1, Pallas kernels, merge(): pl.pallas_call(merge_kernel, in_specs=[pl.BlockSpec(memory_space=pltpu.SM...  1.41 us
    pallas_call x1, Pallas kernels, phases(): pl.pallas_call(phases_kernel, in_specs=[pl.BlockSpec(memory_space=pltpu.S...  1.11 us
  transfers between devices with their start and end apart: 2, of which 0 were waited for; matrix products, arithmetic and copies ran while one was open for 2% of the time, Pallas kernels for 5%

profile of v4, /device:TPU:1, one launch (start us, length us, event | category | flops | bytes accessed | tf_op | source)
XLA Modules:
  0.0 54.7 jit_solution(3920603458992001648)
XLA Ops:
  0.0 3.5 %compress.1 = (bf16[32,2,8,256]{3,2,1,0:T(8,128)(2,1)}, f32[8,128]{1,0:T(8,128)}) custom-call(bf16[2,1,64,4096]{3,2,1,0:T(8,128)(2,1)} %echo_hbm.1, bf16[2,256,1024]{2,1,0:T(8,128)(2,1)} %constant.32.clone.odd_hbm, bf16[4,128,512]{2,1,0:T(8,128)(2,1)} %constant.33.clone.even_hbm), custom_call_target="tpu_custom_call" | custom-call | flops 402653184 | bytes 4194304 | tf_op jit(solution)/shard_map/compress/pallas_call | solution.py:195
  3.5 0.0 copy-start.5
  3.5 17.8 %all-to-all-start = ((bf16[64,8,256]{2,1,0:T(8,128)(2,1)}), bf16[64,8,256]{2,1,0:T(8,128)(2,1)S(1)}, u32[]{:S(2)}, u32[]{:S(2)}) async-start(bf16[64,8,256]{2,1,0:T(8,128)(2,1)} %bitcast.7), calls=%async_computation | async-start | bytes 524288 | tf_op jit(solution)/shard_map/all_to_all | solution.py:618
  22.6 0.1 pad.6.clone
  22.6 0.1 pad.7.clone
  22.7 0.0 copy-done.5
  22.7 0.1 broadcast_in_dim.48
  22.8 0.5 copy-done.3
  23.3 3.1 %collective-permute-start = (f32[8,128]{1,0:T(8,128)S(1)}, f32[8,128]{1,0:T(8,128)S(1)}, u32[]{:S(2)}, u32[]{:S(2)}) collective-permute-start(f32[8,128]{1,0:T(8,128)S(1)} %maximum_add_fusion.own_ref), channel_id=1, source_target_pairs={{0,8},{8,0},{16,24},{24,16},{32,40},{40,32},{48,56},{56,48},{64,72... | collective-permute-start | bytes 12296 | tf_op jit(solution)/shard_map/ppermute | solution.py:628
  26.4 0.0 copy-start.4
  26.4 0.7 %copy-done.4 = f32[512]{0:T(512)S(1)} copy-done((f32[512]{0:T(512)S(1)}, f32[512]{0:T(512)}, u32[]{:S(2)}) %copy-start.4) | copy-done | bytes 2072
  27.1 0.1 cosine_multiply_fusion
  27.2 0.1 stack.17
  27.3 0.1 stack.18
  27.4 0.0 copy-done.2
  27.4 0.4 reshape.16.filter_ref
  27.8 0.2 copy-done.6
  28.0 0.1 select_reduce_fusion
  28.2 0.1 pad_add_fusion.scalars
  28.2 0.1 broadcast_in_dim.47.gain_ref
  28.3 0.0 copy-done
  28.3 1.6 %tables.1 = (f32[2,128,128]{2,1,0:T(8,128)S(1)}, bf16[256,512]{1,0:T(8,128)(2,1)S(1)}, f32[256,256]{1,0:T(8,128)S(1)}, f32[8,32,128]{2,1,0:T(8,128)S(1)}, f32[2,256,256]{2,1,0:T(8,128)S(1)}) custom-call(s32[18]{0:T(128)S(1)} %pad_add_fusion.scalars, f32[2,2,8,128]{3,2,1,0:T(8,128)S(1)} %broadcast_in_dim.47.gain_ref, f32[256,256]{1,0:T(8,128)S(1)} %copy-done, ...), custom_call_target="tpu_custom_call" | custom-call | flops 268435456 | bytes 2097152 | tf_op jit(solution)/shard_map/tables/pallas_call | solution.py:390
  29.9 0.0 copy-start.1
  30.0 0.0 collective-permute-done.other_ref
  30.0 1.1 %phases.1 = (f32[8,32,128]{2,1,0:T(8,128)S(1)}, f32[8,32,128]{2,1,0:T(8,128)S(1)}, f32[2,3,8,128]{3,2,1,0:T(8,128)S(1)}) custom-call(s32[18]{0:T(128)S(1)} %pad_add_fusion.scalars, f32[8,128]{1,0:T(8,128)S(1)} %maximum_add_fusion.own_ref, f32[8,128]{1,0:T(8,128)S(1)} %collective-permute-done.other_ref), custom_call_target="tpu_custom_call" | custom-call | flops 16777216 | bytes 1048576 | tf_op jit(solution)/shard_map/phases/pallas_call | solution.py:435
  31.1 0.0 all-to-all-done.turned_ref
  31.1 0.0 copy-done.1
  31.1 0.6 %spectra.1 = bf16[16,32,256]{2,1,0:T(8,128)(2,1)S(1)} custom-call(bf16[64,8,256]{2,1,0:T(8,128)(2,1)S(1)} %all-to-all-done.turned_ref, bf16[256,512]{1,0:T(8,128)(2,1)S(1)} %copy-done.1, f32[2,256,256]{2,1,0:T(8,128)S(1)} %get-tuple-element.16.twiddle_ref, f32[2,3,8,128]{3,2,1,0:T(8,128)S(1)} %get-tuple-element.18.after_ref.mask_ref), custom_call_target="tpu_custom_call" | custom-call | flops 201326592 | bytes 2097152 | tf_op jit(solution)/shard_map/spectra/pallas_call | solution.py:301
  31.7 11.8 %all_to_all.15.gathered_ref = bf16[16,32,256]{2,1,0:T(8,128)(2,1)S(1)} all-to-all(bf16[16,32,256]{2,1,0:T(8,128)(2,1)S(1)} %spectra.1), channel_id=1, replica_groups={{15,14,13,12,11,10,9,8,7,6,5,4,3,2,1,0},{31,30,29,28,27,26,25,24,23,22,..., dimensions={0} | all-to-all | bytes 524288 | tf_op jit(solution)/shard_map/all_to_all | solution.py:608
  43.6 1.4 %merge.1 = bf16[16,16,256]{2,1,0:T(8,128)(2,1)S(1)} custom-call(s32[18]{0:T(128)S(1)} %pad_add_fusion.scalars, bf16[16,32,256]{2,1,0:T(8,128)(2,1)S(1)} %all_to_all.15.gathered_ref, f32[2,128,128]{2,1,0:T(8,128)S(1)} %get-tuple-element.19.filt_ref, f32[8,32,128]{2,1,0:T(8,128)S(1)} %get-tuple-element.20.cos_ref, ...), custom_call_target="tpu_custom_call" | custom-call | flops 16777216 | bytes 2097152 | tf_op jit(solution)/shard_map/merge/pallas_call | solution.py:526
  45.0 8.7 %all_to_all.16.combined_ref = bf16[16,16,256]{2,1,0:T(8,128)(2,1)S(1)} all-to-all(bf16[16,16,256]{2,1,0:T(8,128)(2,1)S(1)} %merge.1), channel_id=1, replica_groups={{15,14,13,12,11,10,9,8,7,6,5,4,3,2,1,0},{31,30,29,28,27,26,25,24,23,22,..., dimensions={0} | all-to-all | bytes 262144 | tf_op jit(solution)/shard_map/all_to_all | solution.py:608
  53.7 1.0 %image.1 = f32[2,8,4096]{2,1,0:T(8,128)} custom-call(bf16[16,16,256]{2,1,0:T(8,128)(2,1)S(1)} %all_to_all.16.combined_ref, bf16[256,512]{1,0:T(8,128)(2,1)S(1)} %get-tuple-element.23.lanes_ref, f32[256,256]{1,0:T(8,128)S(1)} %get-tuple-element.24.twiddle_ref), custom_call_target="tpu_custom_call" | custom-call | flops 67108864 | bytes 2097152 | tf_op jit(solution)/shard_map/image/pallas_call | solution.py:560
  (8 shorter events, 0.0 us)
Async XLA Ops:
  0.0 27.4 %copy-start.2 = (bf16[8,8,2,4096]{3,2,1,0:T(2,128)(2,1)S(1)}, bf16[8,8,2,4096]{3,2,1,0:T(2,128)(2,1)}, u32[]{:S(2)}) copy-start(bf16[8,8,2,4096]{3,2,1,0:T(2,128)(2,1)} %param.17) | copy-start | bytes 3145732
  3.5 19.2 %copy-start.5 = (f32[8]{0:T(128)S(1)}, f32[8]{0:T(128)}, u32[]{:S(2)}) copy-start(f32[8]{0:T(128)} %param.13) | copy-start | bytes 100
  3.5 27.6 %all-to-all-start = ((bf16[64,8,256]{2,1,0:T(8,128)(2,1)}), bf16[64,8,256]{2,1,0:T(8,128)(2,1)S(1)}, u32[]{:S(2)}, u32[]{:S(2)}) async-start(bf16[64,8,256]{2,1,0:T(8,128)(2,1)} %bitcast.7), calls=%async_computation | async-start | bytes 524288 | tf_op jit(solution)/shard_map/all_to_all | solution.py:618
  22.6 0.7 %copy-start.3 = (f32[8,128]{1,0:T(8,128)S(1)}, f32[8,128]{1,0:T(8,128)}, u32[]{:S(2)}) copy-start(f32[8,128]{1,0:T(8,128)} %get-tuple-element.17) | copy-start | bytes 12292
  23.3 6.7 %collective-permute-start = (f32[8,128]{1,0:T(8,128)S(1)}, f32[8,128]{1,0:T(8,128)S(1)}, u32[]{:S(2)}, u32[]{:S(2)}) collective-permute-start(f32[8,128]{1,0:T(8,128)S(1)} %maximum_add_fusion.own_ref), channel_id=1, source_target_pairs={{0,8},{8,0},{16,24},{24,16},{32,40},{40,32},{48,56},{56,48},{64,72... | collective-permute-start | bytes 12296 | tf_op jit(solution)/shard_map/ppermute | solution.py:628
  26.4 0.7 %copy-start.4 = (f32[512]{0:T(512)S(1)}, f32[512]{0:T(512)}, u32[]{:S(2)}) copy-start(f32[512]{0:T(512)} %param.12) | copy-start | bytes 6148
  27.4 0.7 %copy-start.6 = (s32[8]{0:T(128)S(1)}, s32[8]{0:T(128)}, u32[]{:S(2)}) copy-start(s32[8]{0:T(128)} %param.16) | copy-start | bytes 100
  27.4 1.0 %copy-start = (f32[256,256]{1,0:T(8,128)S(1)}, f32[256,256]{1,0:T(8,128)}, u32[]{:S(2)}) copy-start(f32[256,256]{1,0:T(8,128)} %constant.34.clone.turns_ref) | copy-start | bytes 786436
  29.9 1.1 %copy-start.1 = (bf16[256,512]{1,0:T(8,128)(2,1)S(1)}, bf16[256,512]{1,0:T(8,128)(2,1)}, u32[]{:S(2)}) copy-start(bf16[256,512]{1,0:T(8,128)(2,1)} %constant.35.clone.lanes_ref) | copy-start | bytes 786436
